TPU v7x, 128 devices: a whole 4x4x4 slice. The times are simulated.
128 devices in a mesh: ctx: 32 (over y, z, core), exp: 4 (over x).
Axes of the slice: x: 4, y: 4, z: 4, core: 2. Of those that a mesh axis runs over, the one named last changes fastest.
Arguments:
- queries: bfloat16 [4096, 6144], P('ctx', 'exp'), may hold values from -0.3984375 to 0.3984375
- keys: bfloat16 [4096, 6144], P('ctx', 'exp'), may hold values from -0.3984375 to 0.3984375
- values: bfloat16 [4096, 6144], P('ctx', 'exp'), may hold values from -0.3984375 to 0.3984375
- log_decay: float32 [48, 4096], P('exp', 'ctx'), may hold values from -1 to 0, as said below
- moe_input: bfloat16 [4096, 6144], P('ctx', 'exp'), may hold values from -6 to 6
- out_grad: bfloat16 [4096, 6144], P('ctx', 'exp'), may hold values from -6 to 6
- expert_ids: int32 [4096, 2], P('ctx'), may hold values from 0 to 31, all different within a row; in each aligned block of 128 rows (0 to 127, 128 to 255, ...) at most 9 rows name the same one
- route_gates: float32 [4096, 2], P('ctx'), may hold values from 0.2 to 1
- w_gate: bfloat16 [4, 6144, 8192], P('exp', None, 'ctx'), may hold values from -0.078125 to 0.078125
- w_up: bfloat16 [4, 6144, 8192], P('exp', None, 'ctx'), may hold values from -0.078125 to 0.078125
- w_down: bfloat16 [4, 8192, 6144], P('exp', 'ctx'), may hold values from -0.0625 to 0.0625
Outputs:
- query_grad: bfloat16 [4096, 6144], P('ctx', 'exp')
- key_grad: bfloat16 [4096, 6144], P('ctx', 'exp')
- value_grad: bfloat16 [4096, 6144], P('ctx', 'exp')
- gate_grad: bfloat16 [4, 6144, 8192], P('exp', None, 'ctx')
- up_grad: bfloat16 [4, 6144, 8192], P('exp', None, 'ctx')
- down_grad: bfloat16 [4, 8192, 6144], P('exp', 'ctx')
Inputs may be any that keep to these rules, and one draw needn't show every extreme that they name: `expert_ids`: each row names 2 different experts. In each aligned block of 128 rows (the rows of one index of ctx) no expert is named by more than 9 rows. `log_decay`: every entry is negative.
All inputs are finite; a program needn't handle non-finite values.
Results may differ from a plain program's by a relative error of at most 0.02.
Values may be sent and summed in bfloat16 or wider, within the bound.
A program may use at most 192 MiB of HBM per device.

v0:
```python
import jax
import jax.numpy as jnp
from jax import lax
from jax.sharding import PartitionSpec as P

TOP = 2
CAP = 9


def entering(value, axis, join, neutral, backward):
    count = lax.axis_size(axis)
    place = lax.axis_index(axis)
    ahead = count - 1 - place if backward else place
    gathered = jax.tree.map(
        lambda a, kind: lax.all_gather(a.astype(kind), axis), value, (jnp.bfloat16, jnp.bfloat16)
    )
    state = jax.tree.map(lambda a, e: jnp.zeros_like(a) + jnp.asarray(e, a.dtype), value, neutral)

    def one(step, state):
        source = count - 1 - step if backward else step
        return join(
            state,
            jax.tree.map(
                lambda a, own: lax.dynamic_index_in_dim(a, source, 0, False).astype(own.dtype),
                gathered,
                value,
            ),
        )

    return lax.fori_loop(0, ahead, one, state)


def multiply(form, left, right):
    return jnp.einsum(form, left, right, preferred_element_type=jnp.float32)


def route_places(expert_ids, flight):
    flat_ids = expert_ids.reshape(-1)
    owners = jnp.arange(flight, dtype=jnp.int32)
    onehot = (flat_ids[:, None] == owners[None, :]).astype(jnp.float32)
    before = jnp.cumsum(onehot, axis=0) - onehot
    slot_rank = jnp.sum(before * onehot, axis=1).astype(jnp.int32)
    live_route = jnp.sum(onehot, axis=1) > 0.5
    places = jnp.where(live_route, flat_ids * CAP + slot_rank, -1)
    return places.reshape(expert_ids.shape)


def selectors(places, flight):
    slot_ids = jnp.arange(flight * CAP, dtype=jnp.int32)
    return [
        (places[:, route_index][None, :] == slot_ids[:, None]).astype(jnp.bfloat16)
        for route_index in range(TOP)
    ]


def dispatch(pickers, sources):
    summed = jnp.zeros((pickers[0].shape[0], sources[0].shape[1]), jnp.float32)
    for chooser, source in zip(pickers, sources):
        summed = summed + jnp.dot(chooser, source, preferred_element_type=jnp.float32)
    return summed.astype(jnp.bfloat16)


def combine_back(pickers, slots_back, base_grad):
    summed = base_grad.astype(jnp.float32)
    for chooser in pickers:
        summed = summed + lax.dot_general(
            chooser, slots_back, (((0,), (0,)), ((), ())), preferred_element_type=jnp.float32
        )
    return summed.astype(jnp.bfloat16)


def expert_backward(inputs, grads, gate_w, up_w, down_w):
    gate_pre = jnp.dot(inputs, gate_w, preferred_element_type=jnp.float32)
    up_pre = jnp.dot(inputs, up_w, preferred_element_type=jnp.float32)
    sigmoid_gate = jax.nn.sigmoid(gate_pre)
    active = gate_pre * sigmoid_gate
    hidden = (active * up_pre).astype(jnp.bfloat16)
    hidden_grad = lax.dot_general(
        grads, down_w, (((1,), (1,)), ((), ())), preferred_element_type=jnp.float32
    )
    down_part = lax.dot_general(
        hidden, grads, (((0,), (0,)), ((), ())), preferred_element_type=jnp.float32
    ).astype(jnp.bfloat16)
    gate_act = (
        hidden_grad * up_pre * sigmoid_gate * (1.0 + gate_pre * (1.0 - sigmoid_gate))
    ).astype(jnp.bfloat16)
    up_act = (hidden_grad * active).astype(jnp.bfloat16)
    gate_part = lax.dot_general(
        inputs, gate_act, (((0,), (0,)), ((), ())), preferred_element_type=jnp.float32
    ).astype(jnp.bfloat16)
    up_part = lax.dot_general(
        inputs, up_act, (((0,), (0,)), ((), ())), preferred_element_type=jnp.float32
    ).astype(jnp.bfloat16)
    return (gate_act, up_act, gate_part, up_part, down_part)


def decay_tables(decay):
    running = jnp.cumsum(decay, axis=1)
    block_total = running[:, -1]
    length = decay.shape[1]
    lower = (jnp.arange(length)[:, None] >= jnp.arange(length)[None, :])[None]
    spread = running[:, :, None] - running[:, None, :]
    weights = jnp.where(lower, jnp.exp(jnp.where(lower, spread, 0.0)), 0.0)
    return (running, block_total, weights)


def local_state(block_total, running, key_half, value_half):
    scale = jnp.exp(block_total[:, None] - running).T[:, :, None]
    decayed = (scale * key_half.astype(jnp.float32)).astype(jnp.bfloat16)
    return multiply("shd,she->hde", decayed, value_half)


def grad_state(running, query_half, grad_half):
    decayed = (jnp.exp(running).T[:, :, None] * query_half.astype(jnp.float32)).astype(jnp.bfloat16)
    return multiply("thd,the->hde", decayed, grad_half)


def block_grads(
    weights, running, block_total, query_half, key_half, value_half, grad_half, state_in, state_grad
):
    mixed = (multiply("the,she->hts", grad_half, value_half) * weights).astype(jnp.bfloat16)
    scores = (multiply("thd,shd->hts", query_half, key_half) * weights).astype(jnp.bfloat16)
    front = jnp.exp(running).T[:, :, None]
    tail = jnp.exp(block_total[:, None] - running).T[:, :, None]
    q_grad = multiply("hts,shd->thd", mixed, key_half) + front * multiply(
        "the,hde->thd", grad_half, state_in
    )
    k_grad = multiply("hts,thd->shd", mixed, query_half) + tail * multiply(
        "she,hde->shd", value_half, state_grad
    )
    v_grad = multiply("hts,the->she", scores, grad_half) + tail * multiply(
        "shd,hde->she", key_half, state_grad
    )
    return (q_grad, k_grad, v_grad)


def join_states(earlier, later):
    return (earlier[0] * later[0], later[0][:, None, None] * earlier[1] + later[1])


def on_device(
    queries,
    keys,
    values,
    log_decay,
    moe_input,
    out_grad,
    expert_ids,
    route_gates,
    w_gate,
    w_up,
    w_down,
):
    row_count, feat_width = queries.shape
    head_count = log_decay.shape[0]
    head_dim = feat_width // head_count
    flight = lax.axis_size("exp")
    running, block_total, weights = decay_tables(log_decay)
    query_half = queries.reshape(row_count, head_count, head_dim)
    key_half = keys.reshape(row_count, head_count, head_dim)
    value_half = values.reshape(row_count, head_count, head_dim)
    own_state = local_state(block_total, running, key_half, value_half)
    decay_factor = jnp.exp(block_total)
    identity = (jnp.ones_like(decay_factor), jnp.zeros_like(own_state))
    state_in = entering((decay_factor, own_state), "ctx", join_states, identity, False)[1]
    state_in = state_in.astype(jnp.bfloat16)
    places = route_places(expert_ids, flight)
    pickers = selectors(places, flight)
    scaled = [
        (route_gates[:, route_index : route_index + 1] * out_grad).astype(jnp.bfloat16)
        for route_index in range(TOP)
    ]
    slot_inputs = dispatch(pickers, [moe_input] * TOP).reshape(flight, CAP, feat_width)
    slot_grads = dispatch(pickers, scaled).reshape(flight, CAP, feat_width)
    spread = (
        lax.all_gather(slot_inputs, "ctx", axis=1, tiled=True),
        lax.all_gather(slot_grads, "ctx", axis=1, tiled=True),
    )
    owned = (
        lax.all_to_all(spread[0], "exp", split_axis=0, concat_axis=2, tiled=True),
        lax.all_to_all(spread[1], "exp", split_axis=0, concat_axis=2, tiled=True),
    )
    expert_inputs, expert_grads = (owned[0][0], owned[1][0])
    gate_w = w_gate[0]
    up_w = w_up[0]
    gate_act, up_act, gate_part, up_part, down_part = expert_backward(
        expert_inputs, expert_grads, gate_w, up_w, w_down[0]
    )
    summed = lax.dot_general(
        gate_act, gate_w, (((1,), (1,)), ((), ())), preferred_element_type=jnp.float32
    )
    slot_sums = lax.psum_scatter(
        (
            summed
            + lax.dot_general(
                up_act, up_w, (((1,), (1,)), ((), ())), preferred_element_type=jnp.float32
            )
        ).astype(jnp.bfloat16),
        "ctx",
        scatter_dimension=0,
        tiled=True,
    )
    slot_back = slot_sums[None]
    returned = lax.all_to_all(slot_back, "exp", split_axis=2, concat_axis=0, tiled=True)
    attn_grad = combine_back(pickers, returned.reshape(flight * CAP, feat_width), out_grad)
    grad_half = attn_grad.reshape(row_count, head_count, head_dim)
    own_grad = grad_state(running, query_half, grad_half)
    state_grad = entering((decay_factor, own_grad), "ctx", join_states, identity, True)[1]
    state_grad = state_grad.astype(jnp.bfloat16)
    q_grad, k_grad, v_grad = block_grads(
        weights,
        running,
        block_total,
        query_half,
        key_half,
        value_half,
        grad_half,
        state_in,
        state_grad,
    )
    query_grad = q_grad.reshape(row_count, feat_width).astype(jnp.bfloat16)
    key_grad = k_grad.reshape(row_count, feat_width).astype(jnp.bfloat16)
    value_grad = v_grad.reshape(row_count, feat_width).astype(jnp.bfloat16)
    return (query_grad, key_grad, value_grad, gate_part[None], up_part[None], down_part[None])


def solution(mesh):
    return jax.shard_map(
        on_device,
        mesh=mesh,
        in_specs=(
            P("ctx", "exp"),
            P("ctx", "exp"),
            P("ctx", "exp"),
            P("exp", "ctx"),
            P("ctx", "exp"),
            P("ctx", "exp"),
            P("ctx", None),
            P("ctx", None),
            P("exp", None, "ctx"),
            P("exp", None, "ctx"),
            P("exp", "ctx", None),
        ),
        out_specs=(
            P("ctx", "exp"),
            P("ctx", "exp"),
            P("ctx", "exp"),
            P("exp", None, "ctx"),
            P("exp", None, "ctx"),
            P("exp", "ctx", None),
        ),
        check_vma=False,
    )
```

profile of v0, /device:TPU:1, one launch (start us, length us, event | category | flops | bytes accessed | tf_op | source)
XLA Modules:
  0.0 492.9 jit_solution(1901437644045196289)
XLA Ops:
  18.7 45.4 %all-gather.10.cloned.1.call-done = bf16[4,288,1536]{2,0,1:T(4,128)(2,1)} async-done(((bf16[4,9,1536]{2,0,1:T(4,128)(2,1)}), bf16[4,288,1536]{2,0,1:T(4,128)(2,1)}) %all-gather.10.cloned.1.call-update) | async-done | bytes 3538960 | tf_op jit(solution)/shard_map/all_gather | solution.py:176
  64.1 4.5 copy.180
  68.6 4.7 all-to-all-start.1
  73.4 38.5 %all-gather.8.cloned.1.call-done = bf16[4,288,1536]{2,0,1:T(4,128)(2,1)} async-done(((bf16[4,9,1536]{2,0,1:T(4,128)(2,1)}), bf16[4,288,1536]{2,0,1:T(4,128)(2,1)}) %all-gather.8.cloned.1.call-update) | async-done | bytes 3538960 | tf_op jit(solution)/shard_map/all_gather | solution.py:177
  111.9 4.4 copy.177
  116.3 4.8 all-to-all-start
  121.2 4.7 copy.181
  128.7 1.4 copy-done.10
  130.1 1.8 fusion.9
  131.9 30.9 %all-to-all-done = bf16[4,288,1536]{2,1,0:T(8,128)(2,1)} async-done(((bf16[4,288,1536]{2,1,0:T(8,128)(2,1)}), bf16[4,288,1536]{2,1,0:T(8,128)(2,1)}, u32[]{:S(2)}, u32[]{:S(2)}) %all-to-all-start) | async-done | bytes 3538976 | tf_op jit(solution)/shard_map/all_to_all | solution.py:181
  162.8 4.7 copy.178
  172.9 3.1 fusion
  181.0 103.7 %all-reduce.4.cloned.1.call-done = bf16[288,6144]{1,0:T(8,128)(2,1)} async-done(((bf16[288,6144]{1,0:T(8,128)(2,1)}), bf16[288,6144]{1,0:T(8,128)(2,1)}) %all-reduce.4.cloned.1.call-update) | async-done | bytes 3538960
  284.7 1.7 dynamic-slice_bitcast_fusion
  286.4 5.9 %copy.182 = bf16[1,9,6144]{1,0,2:T(2,128)(2,1)S(1)} copy(bf16[1,9,6144]{2,1,0:T(8,128)(2,1)} %dynamic-slice_bitcast_fusion) | data formatting | bytes 221184 | tf_op jit(solution)/shard_map/broadcast_in_dim | solution.py:203
  292.9 34.4 %reduce.4 = bf16[6144,9]{1,0:T(8,128)(2,1)} reduce(bf16[6144,1,9]{2,1,0:T(2,128)(2,1)S(1)} %bitcast.156, bf16[]{:T(256)} %broadcast.49), dimensions={1}, to_apply=%bitcast.112.reduce_sub_computation | reduce | bytes 221186
  327.3 4.3 reshape.144
  331.5 4.0 all-to-all-start.2
  335.5 1.9 copy.192
  337.4 2.9 all-to-all-done.2
  340.3 3.9 reshape.145
  344.2 4.8 copy.183
  350.2 1.3 convolution_add_fusion.2
  354.9 65.3 %all-reduce = bf16[384]{0:T(512)(128)(2,1)S(1)} all-reduce(bf16[384]{0:T(512)(128)(2,1)S(1)} %dynamic-update-slice), channel_id=2, replica_groups=mesh['ctx'=32,'exp'=4] {'ctx'}, use_global_device_ids=true, to_apply=%add | all-reduce | flops 384 | bytes 1536
  420.4 5.7 %fusion.3 = bf16[1,256,6144]{2,1,0:T(8,128)(2,1)} fusion(bf16[288,6144]{1,0:T(8,128)(2,1)} %bitcast.153, f32[288,256]{1,0:T(8,128)S(1)} %copy-done.20, f32[288,256]{1,0:T(8,128)S(1)} %copy-done.18), kind=kOutput, calls=%fused_computation.11 | convolution fusion | flops 907984896 | bytes 7274496 | tf_op jit(solution)/shard_map/dot_general | solution.py:81
  426.1 3.5 fusion.1
  429.6 3.5 fusion.2
  436.6 37.4 %while.27 = (s32[]{:T(128)}, f32[12,128,128]{2,1,0:T(8,128)S(1)}, s32[]{:T(128)}, bf16[32,12]{1,0:T(8,128)(2,1)S(1)}, bf16[32,12,128,128]{3,2,1,0:T(8,128)(2,1)}...) while((s32[]{:T(128)}, f32[12,128,128]{2,1,0:T(8,128)S(1)}, s32[]{:T(128)}, ...), condition=%wide.region_9.10_spmd, body=%wide.region_8.9_spmd.sunk | while | flops 589842 | bytes 1966347 | solution.py:30
  476.2 2.5 fusion.19
  478.7 2.7 fusion.23
  481.4 1.9 copy.201
  483.3 1.6 fusion.24
  (196 shorter events, 72.5 us)
Async XLA Ops:
  7.2 119.7 %copy-start = (bf16[1,6144,256]{2,1,0:T(8,128)(2,1)S(1)}, bf16[1,6144,256]{2,1,0:T(8,128)(2,1)}, u32[]{:S(2)}) copy-start(bf16[1,6144,256]{2,1,0:T(8,128)(2,1)} %param.23) | copy-start | bytes 9437188
  7.2 56.9 %all-gather.10.cloned.1.call-start = ((), (), s32[]{:S(2)}) async-start(), calls=%async_computation.4 | async-start | bytes 3649536 | tf_op jit(solution)/shard_map/all_gather | solution.py:176
  11.3 57.3 %copy-start.26 = (s32[128]{0:T(128)}, s32[128]{0:T(128)S(1)}, u32[]{:S(2)}) copy-start(s32[128]{0:T(128)S(1)} %get-tuple-element.206) | copy-start | bytes 1540
  11.3 57.3 %copy-start.27 = (s32[128]{0:T(128)}, s32[128]{0:T(128)S(1)}, u32[]{:S(2)}) copy-start(s32[128]{0:T(128)S(1)} %get-tuple-element.207) | copy-start | bytes 1540
  14.5 97.4 %all-gather.8.cloned.1.call-start = ((), (), s32[]{:S(2)}) async-start(), calls=%async_computation.3 | async-start | bytes 3649536 | tf_op jit(solution)/shard_map/all_gather | solution.py:177
  68.6 47.6 %all-to-all-start.1 = ((bf16[4,288,1536]{2,1,0:T(8,128)(2,1)}), bf16[4,288,1536]{2,1,0:T(8,128)(2,1)}, u32[]{:S(2)}, u32[]{:S(2)}) async-start(bf16[4,288,1536]{2,1,0:T(8,128)(2,1)} %copy.180), calls=%async_computation.1 | async-start | bytes 7077888 | tf_op jit(solution)/shard_map/all_to_all | solution.py:180
  116.3 46.5 %all-to-all-start = ((bf16[4,288,1536]{2,1,0:T(8,128)(2,1)}), bf16[4,288,1536]{2,1,0:T(8,128)(2,1)}, u32[]{:S(2)}, u32[]{:S(2)}) async-start(bf16[4,288,1536]{2,1,0:T(8,128)(2,1)} %copy.177), calls=%async_computation | async-start | bytes 7077888 | tf_op jit(solution)/shard_map/all_to_all | solution.py:181
  121.0 163.7 %all-reduce.4.cloned.1.call-start = ((), (), s32[]{:S(2)}) async-start(), calls=%async_computation.7 | async-start | bytes 7077888
  126.9 1.8 copy-start.4
  126.9 3.2 copy-start.10
  130.1 38.4 %copy-start.17 = (f32[288,256]{1,0:T(8,128)}, f32[288,256]{1,0:T(8,128)S(1)}, u32[]{:S(2)}) copy-start(f32[288,256]{1,0:T(8,128)S(1)} %fusion.6) | copy-start | bytes 884740
  167.5 2.2 copy-start.29
  168.4 2.4 copy-start.3
  170.9 2.0 copy-start.11
  176.0 1.5 copy-start.25
  176.0 3.7 copy-start.28
  176.0 257.5 %all-gather.12.cloned.1.call-start = ((), (), s32[]{:S(2)}) async-start(), calls=%async_computation.5 | async-start | bytes 12976128 | tf_op jit(solution)/shard_map/all_gather | solution.py:15
  177.5 107.2 %copy-start.6 = (bf16[128,1536]{0,1:T(8,128)(2,1)}, bf16[128,1536]{0,1:T(8,128)(2,1)S(1)}, u32[]{:S(2)}) copy-start(bf16[128,1536]{0,1:T(8,128)(2,1)S(1)} %copy.186) | copy-start | bytes 1179652
  331.5 8.8 %all-to-all-start.2 = ((bf16[4,2,6912]{2,1,0:T(2,128)(2,1)}), bf16[4,2,6912]{2,1,0:T(2,128)(2,1)}, u32[]{:S(2)}, u32[]{:S(2)}) async-start(bf16[4,2,6912]{2,1,0:T(2,128)(2,1)} %reshape.144), calls=%async_computation.2 | async-start | bytes 221184 | tf_op jit(solution)/shard_map/all_to_all | solution.py:204
  335.5 101.0 %all-gather.14.cloned.1.call-start = ((), (), s32[]{:S(2)}) async-start(), calls=%async_computation.6 | async-start | bytes 12976128 | tf_op jit(solution)/shard_map/all_gather | solution.py:15
  349.0 3.7 copy-start.8
  349.0 3.7 copy-start.23
  349.0 71.3 %copy-start.18 = (f32[288,256]{1,0:T(8,128)S(1)}, f32[288,256]{1,0:T(8,128)}, u32[]{:S(2)}) copy-start(f32[288,256]{1,0:T(8,128)} %copy-done.17) | copy-start | bytes 884740
  349.0 71.3 %copy-start.20 = (f32[288,256]{1,0:T(8,128)S(1)}, f32[288,256]{1,0:T(8,128)}, u32[]{:S(2)}) copy-start(f32[288,256]{1,0:T(8,128)} %fusion.9) | copy-start | bytes 884740
  352.7 82.2 %copy-start.9 = (bf16[128,1536]{0,1:T(8,128)(2,1)}, bf16[128,1536]{0,1:T(8,128)(2,1)S(1)}, u32[]{:S(2)}) copy-start(bf16[128,1536]{0,1:T(8,128)(2,1)S(1)} %copy.185) | copy-start | bytes 1179652
  420.3 12.7 %copy-start.24 = (pred[128,128]{1,0:T(8,128)(4,1)}, pred[128,128]{1,0:T(8,128)(4,1)S(1)}, u32[]{:S(2)}) copy-start(pred[128,128]{1,0:T(8,128)(4,1)S(1)} %iota_compare_fusion) | copy-start | bytes 49156
  420.4 5.7 %copy-start.5 = (bf16[36,8,4,1536]{3,1,2,0:T(8,128)(2,1)S(1)}, bf16[36,8,4,1536]{3,1,2,0:T(8,128)(2,1)}, u32[]{:S(2)}) copy-start(bf16[36,8,4,1536]{3,1,2,0:T(8,128)(2,1)} %copy-done.4) | copy-start | bytes 10616836
  420.4 5.7 %copy-start.22 = (bf16[288,256]{1,0:T(8,128)(2,1)S(1)}, bf16[288,256]{1,0:T(8,128)(2,1)}, u32[]{:S(2)}) copy-start(bf16[288,256]{1,0:T(8,128)(2,1)} %copy-done.21) | copy-start | bytes 442372
  426.1 3.5 copy-start.14
  429.6 3.5 copy-start.7
  433.5 1.6 copy-start.12
  476.2 9.8 %copy-start.1 = (bf16[1,6144,256]{2,1,0:T(8,128)(2,1)S(1)}, bf16[1,6144,256]{2,1,0:T(8,128)(2,1)}, u32[]{:S(2)}) copy-start(bf16[1,6144,256]{2,1,0:T(8,128)(2,1)} %param.23) | copy-start | bytes 9437188
  (6 other events, 6.4 us)
Sparse Core Ops, SparseCore 0:
  14.6 49.4 all-gather.9
  67.0 44.8 all-gather.7
  176.2 108.5 all-reduce.3
  287.4 62.9 all-gather.11
  354.0 62.3 all-gather.13
where the time goes:
time: 500 us; the launch traced here: 493 us
  waiting for transfers between devices  222 us (44%)
  other arithmetic  75.2 us (15%)
  blocking collectives  65.3 us (13%)
  local copies, waits for them, and re-layouts  60.3 us (12%)
  matrix products  39.6 us (8%)
  between operations  16 us (3%)
  starting transfers between devices  13.8 us (3%)
    unnamed x6, waiting for transfers between devices  104 us
    unnamed x1, blocking collectives  65.3 us
    all_gather x1, waiting for transfers between devices, on_device(): lax.all_gather(slot_inputs, 'ctx', axis=1, tiled=True)  45.4 us
    all_gather x1, waiting for transfers between devices, on_device(): lax.all_gather(slot_grads, 'ctx', axis=1, tiled=True)  38.5 us
    add x31, other arithmetic, join_states(): later[0][:, None, None] * earlier[1] + later[1]  37.2 us
    unnamed x2, other arithmetic  34.5 us
    all_to_all x1, waiting for transfers between devices, on_device(): lax.all_to_all(spread[1], 'exp', split_axis=0, concat_axis=2, tiled=True)  30.9 us
    unnamed x75, local copies, waits for them, and re-layouts  24.5 us
  transfers between devices with their start and end apart: 8, of which 5 were waited for; matrix products, arithmetic and copies ran while one was open for 21% of the time, Pallas kernels for 0%

commit v1 on v0

v1 whole, which is shorter than its diff:
```python
import jax
import jax.numpy as jnp
from jax import lax
from jax.experimental import pallas as pl
from jax.experimental.pallas import tpu as pltpu
from jax.sharding import PartitionSpec as P

MESH = pl.DeviceIdType.MESH
BF16 = jnp.bfloat16
F32 = jnp.float32

FLIGHT = 4
D = 6144
QUARTER = D // 4
HID = 256
HEADS = 12
HALF_HEADS = HEADS // 2
HD = 128
ROWS = 128
MAIN = 256
SLOTS = 288
REM = 768
WIDE = D + REM
CUT = WIDE // 2
SHARE = 4 * 768 + 384
SHARE_CUT = 1792
BIG = 56 * 1024 * 1024


def dot(a, b):
    return lax.dot_general(a, b, (((1,), (0,)), ((), ())), preferred_element_type=F32)


def dot_nt(a, b):
    return lax.dot_general(a, b, (((1,), (1,)), ((), ())), preferred_element_type=F32)


def dot_tn(a, b):
    return lax.dot_general(a, b, (((0,), (0,)), ((), ())), preferred_element_type=F32)


def iota(shape, dim):
    return lax.broadcasted_iota(jnp.int32, shape, dim)


def aligned(value, by):
    return pl.multiple_of(value, by)


class Place:
    def __init__(self):
        ctx = lax.axis_index("ctx")
        self.x = lax.axis_index("exp")
        self.ctx = ctx
        self.core = lax.rem(ctx, 2)
        self.z = lax.rem(lax.div(ctx, 2), 4)
        self.y = lax.div(ctx, 8)
        self.chip = self.y * 4 + self.z

    def at(self, y=None, z=None, core=None, x=None):
        y = self.y if y is None else y
        z = self.z if z is None else z
        core = self.core if core is None else core
        x = self.x if x is None else x
        return (y * 8 + z * 2 + core, x)

    def sibling(self):
        return self.at(core=1 - self.core)


class Wires:
    def __init__(self, place, send_sems, recv_sems):
        self.place, self.send_sems, self.recv_sems = place, send_sems, recv_sems
        self.names, self.sent = {}, []

    def slot(self, name):
        return self.names.setdefault(name, len(self.names))

    def send(self, name, src, dst, device):
        slot = self.slot(name)
        copy = pltpu.make_async_remote_copy(
            src_ref=src,
            dst_ref=dst,
            send_sem=self.send_sems.at[slot],
            recv_sem=self.recv_sems.at[slot],
            device_id=device,
            device_id_type=MESH,
        )
        copy.start()
        self.sent.append(copy)

    def arrived(self, name, region):
        slot = self.slot(name)
        pltpu.make_async_remote_copy(
            src_ref=region,
            dst_ref=region,
            send_sem=self.send_sems.at[slot],
            recv_sem=self.recv_sems.at[slot],
            device_id=self.place.sibling(),
            device_id_type=MESH,
        ).wait_recv()

    def drain(self):
        for copy in self.sent:
            copy.wait_send()
        self.sent = []


def greet(devices):
    barrier = pltpu.get_barrier_semaphore()
    for device in devices:
        pl.semaphore_signal(barrier, inc=1, device_id=device, device_id_type=MESH)
    pl.semaphore_wait(barrier, len(devices))


def route_masks(small, place):
    ids0, ids1 = small[16:17, :], small[17:18, :]
    gates0, gates1 = small[18:19, :], small[19:20, :]
    wanted = lax.broadcasted_iota(jnp.int32, (8, ROWS), 0).astype(F32)
    first = ids0 == wanted
    second = ids1 == wanted
    onehot = jnp.where(first | second, 1.0, 0.0)
    gates = jnp.where(first, gates0, 0.0) + jnp.where(second, gates1, 0.0)
    before = jnp.where(iota((ROWS, ROWS), 0) < iota((ROWS, ROWS), 1), 1.0, 0.0).astype(BF16)
    rank = dot(onehot.astype(BF16), before)
    rank = jnp.where(onehot > 0.5, rank, -1.0)

    def spread(a):
        return jnp.concatenate([jnp.broadcast_to(a[e : e + 1, :], (16, ROWS)) for e in range(FLIGHT)], axis=0)

    rank, gates = spread(rank), spread(gates)
    row = lax.rem(iota((64, ROWS), 0), 16)
    mine = lax.div(row, 8) == place.core
    slot = lax.rem(row, 8)
    main = jnp.where(mine & (rank == slot.astype(F32)), 1.0, 0.0)
    ninth = jnp.where(mine & (rank == 8.0), 1.0, 0.0)
    return main, ninth, slot, gates


def moe_kernel(
    small_ref, moe_ref, out_grad_ref, wg_hbm, wu_hbm, wd_hbm,
    x_out, g_out, hidden_out, gate_out, up_out, attn_out, decay_out,
    wg, wu, wd, rows, stage, staged, ninth_in, acc, gact, uact,
    part, theirs, fold, ring_a, ring_b, ring_m, ring_p, group, ring2_a, ring2_b, ring2_m, ring2_p,
    final, back, decay, send_sems, recv_sems, local_sems,
):
    here = Place()
    core, other = here.core, 1 - here.core
    wires = Wires(here, send_sems, recv_sems)

    loads = [
        pltpu.make_async_copy(wg_hbm, wg, local_sems.at[0]),
        pltpu.make_async_copy(wu_hbm, wu, local_sems.at[1]),
        pltpu.make_async_copy(wd_hbm, wd, local_sems.at[2]),
    ]
    for load in loads:
        load.start()

    turn = [lax.rem(here.x + d, 4) for d in range(4)]
    turn_y = [lax.rem(here.y + d, 4) for d in range(4)]
    turn_z = [lax.rem(here.z + d, 4) for d in range(4)]
    greet(
        [here.sibling()]
        + [here.at(x=turn[d]) for d in (1, 2, 3)]
        + [here.at(y=turn_y[d]) for d in (1, 2, 3)]
        + [here.at(z=turn_z[d]) for d in (1, 2, 3)]
    )

    small = small_ref[...]
    decay[here.ctx] = jnp.broadcast_to(jnp.sum(small[0:16, :], axis=1, keepdims=True), (16, ROWS))
    wires.send("d", decay.at[here.ctx], decay.at[here.ctx], here.sibling())

    main, ninth, slot, gates = route_masks(small, here)
    pick = main.astype(BF16)
    main_gate = jnp.sum(main * gates, axis=1, keepdims=True)
    ninth_gate = jnp.sum(ninth * gates, axis=1, keepdims=True)
    fold_at = lax.rem(here.x, 2) * 4
    picks = [
        jnp.where(slot == fold_at + b, ninth, 0.0).astype(BF16) for b in range(4)
    ]
    for which, source in enumerate((moe_ref, out_grad_ref)):
        chosen = dot(pick, source[...])
        extra = dot(picks[0], source[:, 0:384])
        for b in range(1, 4):
            extra = extra + dot(picks[b], source[:, 384 * b : 384 * (b + 1)])
        if which:
            chosen, extra = chosen * main_gate, extra * ninth_gate
        stage[which, :, 0:QUARTER] = chosen.astype(BF16)
        stage[which, :, QUARTER:] = extra.astype(BF16)
    wires.send("s", stage.at[other], staged, here.sibling())
    wires.arrived("s", staged)
    stage[core] = (stage[core].astype(F32) + staged[...].astype(F32)).astype(BF16)

    mine = rows.at[core]
    own_rows = pl.ds(aligned(here.chip * 16, 16), 16)
    for d in (1, 2, 3):
        to = pl.ds(aligned(turn[d] * 16, 16), 16)
        wires.send(
            ("x", d),
            stage.at[core, to, 0:QUARTER],
            mine.at[own_rows, pl.ds(aligned(here.x * QUARTER, QUARTER), QUARTER)],
            here.at(x=turn[d]),
        )
        wires.send(("xr", d), stage.at[core, to, QUARTER:], ninth_in.at[here.x], here.at(x=turn[d]))
    kept = pl.ds(aligned(here.x * 16, 16), 16)
    rows[core, own_rows, pl.ds(aligned(here.x * QUARTER, QUARTER), QUARTER)] = stage[core, kept, 0:QUARTER]
    ninth_in[here.x] = stage[core, kept, QUARTER:]

    wires.arrived("d", decay.at[here.at(core=other)[0]])
    pair = decay.at[pl.ds(here.chip * 2, 2)]
    for d in (1, 2, 3):
        wires.send(("dz", d), pair, pair, here.at(z=turn_z[d]))

    for d in (1, 2, 3):
        source = turn[4 - d]
        wires.arrived(("x", d), mine.at[own_rows, pl.ds(aligned(source * QUARTER, QUARTER), QUARTER)])
        wires.arrived(("xr", d), ninth_in.at[source])
    for p in range(2):
        rows[core, own_rows, D + 384 * p : D + 384 * (p + 1)] = (
            ninth_in[2 * p].astype(F32) + ninth_in[2 * p + 1].astype(F32)
        ).astype(BF16)

    first = jnp.where(core == 0, here.z, here.y)
    second = jnp.where(core == 0, here.y, here.z)
    first_step, second_step = jnp.where(core == 0, 1, 4), jnp.where(core == 0, 4, 1)
    fs = [lax.rem(first + d, 4) for d in range(4)]
    ss = [lax.rem(second + d, 4) for d in range(4)]

    def on_first(value):
        return here.at(y=jnp.where(core == 0, here.y, value), z=jnp.where(core == 0, value, here.z))

    def on_second(value):
        return here.at(y=jnp.where(core == 0, value, here.y), z=jnp.where(core == 0, here.z, value))

    left, right, full = pl.ds(0, CUT), pl.ds(CUT, CUT), pl.ds(0, WIDE)

    def tile(i, j, columns=full):
        at = (fs[i] * first_step + ss[j] * second_step) * 16
        return rows.at[core, pl.ds(aligned(at, 16), 16), columns]

    def their_tile(i, j):
        at = (ss[i] * second_step + fs[j] * first_step) * 16
        return rows.at[other, pl.ds(aligned(at, 16), 16), full]

    def share(i, j):
        wires.send(("c", i, j), tile(i, j), tile(i, j), here.sibling())

    def spread_second(i):
        wires.send(("s+", i), tile(i, 0), tile(i, 0), on_second(ss[1]))
        wires.send(("s-", i), tile(i, 0), tile(i, 0), on_second(ss[3]))
        share(i, 0)

    def pass_second(i):
        wires.arrived(("s+", i), tile(i, 3))
        wires.send(("s+l", i), tile(i, 3, left), tile(i, 3, left), on_second(ss[1]))
        share(i, 3)
        wires.arrived(("s-", i), tile(i, 1))
        wires.send(("s-r", i), tile(i, 1, right), tile(i, 1, right), on_second(ss[3]))
        share(i, 1)

    def end_second(i):
        wires.arrived(("s+l", i), tile(i, 2, left))
        wires.arrived(("s-r", i), tile(i, 2, right))
        share(i, 2)

    wires.send("f+", tile(0, 0), tile(0, 0), on_first(fs[1]))
    wires.send("f-", tile(0, 0), tile(0, 0), on_first(fs[3]))
    spread_second(0)
    wires.arrived("f+", tile(3, 0))
    wires.send("f+l", tile(3, 0, left), tile(3, 0, left), on_first(fs[1]))
    wires.arrived("f-", tile(1, 0))
    wires.send("f-r", tile(1, 0, right), tile(1, 0, right), on_first(fs[3]))
    spread_second(3)
    spread_second(1)
    pass_second(0)
    wires.arrived("f+l", tile(2, 0, left))
    wires.arrived("f-r", tile(2, 0, right))
    spread_second(2)
    for d in (1, 2, 3):
        source = turn_z[4 - d]
        wires.arrived(("dz", d), decay.at[pl.ds((here.y * 4 + source) * 2, 2)])
    line = decay.at[pl.ds(here.y * 8, 8)]
    for d in (1, 2, 3):
        wires.send(("dy", d), line, line, here.at(y=turn_y[d]))
    pass_second(3)
    pass_second(1)
    end_second(0)
    pass_second(2)
    end_second(3)
    end_second(1)
    end_second(2)
    for d in (1, 2, 3):
        wires.arrived(("dy", d), decay.at[pl.ds(turn_y[4 - d] * 8, 8)])
    decay_out[...] = decay[...]
    for i in range(4):
        for j in range(4):
            wires.arrived(("c", i, j), their_tile(i, j))

    r0, r1 = iota((MAIN, MAIN), 0), iota((MAIN, MAIN), 1)
    chip_core, grp = lax.rem(r0, 32), lax.div(r0, 32)
    unfold = jnp.where(r1 == chip_core * 8 + grp, 1.0, 0.0).astype(BF16)
    for which in range(2):
        for p in range(2):
            spread = dot(unfold, rows[which, 0:MAIN, D + 384 * p : D + 384 * (p + 1)]).astype(BF16)
            for g in range(8):
                at = (2 * p + g // 4) * QUARTER + (g % 4) * 384
                rows[which, MAIN:SLOTS, at : at + 384] = spread[32 * g : 32 * (g + 1), :]
    stores = [
        pltpu.make_async_copy(rows.at[0, :, 0:D], x_out, local_sems.at[3]),
        pltpu.make_async_copy(rows.at[1, :, 0:D], g_out, local_sems.at[4]),
    ]
    for store in stores:
        store.start()

    for load in loads:
        load.wait()
    acc[...] = jnp.zeros_like(acc)

    def contract(j, _):
        at = pl.ds(aligned(j * 512, 512), 512)
        inputs, grads = rows[0, :, at], rows[1, :, at]
        acc[0] += dot(inputs, wg[at, :])
        acc[1] += dot(inputs, wu[at, :])
        acc[2] += dot_nt(grads, wd[:, at])
        return 0

    lax.fori_loop(0, D // 512, contract, 0)
    gate_pre, up_pre, hidden_grad = acc[0], acc[1], acc[2]
    sig = jax.nn.sigmoid(gate_pre)
    active = gate_pre * sig
    hidden_out[...] = (active * up_pre).astype(BF16)
    gact[...] = (hidden_grad * up_pre * sig * (1.0 + gate_pre * (1.0 - sig))).astype(BF16)
    uact[...] = (hidden_grad * active).astype(BF16)
    gate_out[...] = gact[...]
    up_out[...] = uact[...]

    def slot_part(which, owner):
        y_step, z_step = jnp.where(owner == 0, 4, 1), jnp.where(owner == 0, 1, 4)

        def one(q, _):
            at = pl.ds(aligned(q * QUARTER + owner * 768, 768), 768)
            piece = dot_nt(gact[...], wg[at, :]) + dot_nt(uact[...], wu[at, :])
            piece = piece.astype(BF16)
            columns = pl.ds(aligned(q * 768, 768), 768)
            for k in range(16):
                to = ((k // 4) * y_step + (k % 4) * z_step) * 16
                part[which, pl.ds(aligned(to, 16), 16), columns] = piece[16 * k : 16 * (k + 1), :]
            for b in range(2):
                fold[pl.ds(aligned((q * 2 + b) * 32, 32), 32), :] = piece[MAIN:, 384 * b : 384 * (b + 1)]
            return 0

        lax.fori_loop(0, 4, one, 0)
        position, inside = lax.div(r0, 16), lax.rem(r0, 16)
        chip = jnp.where(owner == 0, position, lax.rem(position, 4) * 4 + lax.div(position, 4))
        source = lax.rem(inside, 8) * 32 + chip * 2 + lax.div(inside, 8)
        refold = jnp.where(r1 == source, 1.0, 0.0).astype(BF16)
        part[which, :, 3072:] = dot(refold, fold[...]).astype(BF16)

    slot_part(1, other)
    wires.send("p", part.at[1], theirs, here.sibling())
    slot_part(0, core)
    wires.arrived("p", theirs)

    def join(j, _):
        at = pl.ds(aligned(j * 16, 16), 16)
        part[0, at, :] = (part[0, at, :].astype(F32) + theirs[at, :].astype(F32)).astype(BF16)
        return 0

    lax.fori_loop(0, 16, join, 0)

    cl, cr = pl.ds(0, SHARE_CUT), pl.ds(SHARE_CUT, SHARE - SHARE_CUT)

    def ring_sum(tag, buffer, height, places, device, in_a, in_b, in_m, in_p, store_result):
        def block(i, columns):
            return buffer.at[pl.ds(aligned(places[i] * height, height), height), columns]

        def add_into(i, columns, arrived_ref):
            at = pl.ds(aligned(places[i] * height, height), height)
            buffer[at, columns] = (buffer[at, columns].astype(F32) + arrived_ref[...].astype(F32)).astype(BF16)

        up, down = device(places[1]), device(places[3])
        wires.send((tag, "a"), block(2, cl), in_a, up)
        wires.send((tag, "b"), block(2, cr), in_b, down)
        wires.send((tag, "mr"), block(1, cr), in_m.at[:, cr], up)
        wires.send((tag, "pl"), block(3, cl), in_p.at[:, cl], down)
        wires.arrived((tag, "a"), in_a)
        add_into(1, cl, in_a)
        wires.send((tag, "ml"), block(1, cl), in_m.at[:, cl], up)
        wires.arrived((tag, "b"), in_b)
        add_into(3, cr, in_b)
        wires.send((tag, "pr"), block(3, cr), in_p.at[:, cr], down)
        wires.arrived((tag, "mr"), in_m.at[:, cr])
        wires.arrived((tag, "pl"), in_p.at[:, cl])
        wires.arrived((tag, "ml"), in_m.at[:, cl])
        wires.arrived((tag, "pr"), in_p.at[:, cr])
        at = pl.ds(aligned(places[0] * height, height), height)
        store_result(
            (buffer[at, :].astype(F32) + in_m[...].astype(F32) + in_p[...].astype(F32)).astype(BF16)
        )

    def keep_group(value):
        group[...] = value

    def keep_final(value):
        final[...] = value

    ring_sum("r1", part.at[0], 64, ss, on_second, ring_a, ring_b, ring_m, ring_p, keep_group)
    ring_sum("r2", group, 16, fs, on_first, ring2_a, ring2_b, ring2_m, ring2_p, keep_final)

    own_back = pl.ds(aligned(here.x * 16, 16), 16)
    for d in (1, 2, 3):
        columns = pl.ds(aligned(turn[d] * 768, 768), 768)
        wires.send(("b", d), final.at[:, columns], back.at[core, own_back, 0:768], here.at(x=turn[d]))
        wires.send(("br", d), final.at[:, 3072:], back.at[core, own_back, 768:], here.at(x=turn[d]))
    back[core, own_back, 0:768] = final[:, pl.ds(aligned(here.x * 768, 768), 768)]
    back[core, own_back, 768:] = final[:, 3072:]
    for d in (1, 2, 3):
        source = pl.ds(aligned(turn[4 - d] * 16, 16), 16)
        wires.arrived(("b", d), back.at[core, source, 0:768])
        wires.arrived(("br", d), back.at[core, source, 768:])
    wires.send("bc", back.at[core], back.at[core], here.sibling())
    wires.arrived("bc", back.at[other])

    for b in range(2):
        chosen = jnp.where(slot == 2 * here.x + b, ninth, 0.0)
        pick_back = jnp.concatenate([main, chosen], axis=0).astype(BF16)
        for h in range(2):
            at = h * 768 + b * 384
            source = jnp.concatenate(
                [back[h, :, 384 * b : 384 * (b + 1)], back[h, :, 768:]], axis=0
            )
            attn_out[:, at : at + 384] = (
                out_grad_ref[:, at : at + 384].astype(F32) + dot_tn(pick_back, source)
            ).astype(BF16)

    for store in stores:
        store.wait()
    wires.drain()


def scan_kernel(
    small_ref, decay_ref, q_ref, k_ref, v_ref, g_ref,
    dq_out, dk_out, dv_out,
    states, sib, totals, z_in, y_in, results, r_in, for_sib, final, turned, kept, send_sems, recv_sems,
):
    here = Place()
    core, other = here.core, 1 - here.core
    wires = Wires(here, send_sems, recv_sems)
    turn_y = [lax.rem(here.y + d, 4) for d in range(4)]
    turn_z = [lax.rem(here.z + d, 4) for d in range(4)]
    greet(
        [here.sibling()]
        + [here.at(y=turn_y[d]) for d in (1, 2, 3)]
        + [here.at(z=turn_z[d]) for d in (1, 2, 3)]
    )

    run = small_ref[0:16, :]
    lane = iota((16, ROWS), 1)
    step = 1
    while step < ROWS:
        run = run + jnp.where(lane >= step, pltpu.roll(run, step, 1), 0.0)
        step *= 2
    turned[...] = jnp.concatenate([run, jnp.zeros((ROWS - 16, ROWS), F32)], axis=0).T
    total = run[:, ROWS - 1 :]

    def head(h):
        at = slice(h * HD, (h + 1) * HD)
        return q_ref[:, at], k_ref[:, at], v_ref[:, at], g_ref[:, at]

    def columns(h):
        front = turned[:, h : h + 1]
        return jnp.exp(front), jnp.exp(total[h : h + 1, :] - front)

    for h in range(HEADS):
        q, k, v, g = head(h)
        front, tail = columns(h)
        decayed_k = (tail * k.astype(F32)).astype(BF16)
        decayed_q = (front * q.astype(F32)).astype(BF16)
        states[0, h] = dot_tn(decayed_k, v).astype(BF16).reshape(4, 32, HD)
        states[1, h] = dot_tn(decayed_q, g).astype(BF16).reshape(4, 32, HD)
    wires.send("s", states.at[:, pl.ds(other * HALF_HEADS, HALF_HEADS)], sib, here.sibling())

    lower = iota((ROWS, ROWS), 0) >= iota((ROWS, ROWS), 1)

    def local(h):
        q, k, v, g = head(h)
        spread = turned[:, h : h + 1] - run[h : h + 1, :]
        w = jnp.where(lower, jnp.exp(jnp.where(lower, spread, 0.0)), 0.0)
        mixed = (dot_nt(g, v) * w).astype(BF16)
        scores = (dot_nt(q, k) * w).astype(BF16)
        kept[0, h] = dot(mixed, k)
        kept[1, h] = dot_tn(mixed, q)
        kept[2, h] = dot_tn(scores, g)

    def log_total(block, h):
        return decay_ref[block, pl.ds(h, 1), :]

    wires.arrived("s", sib)
    even, odd = here.chip * 2, here.chip * 2 + 1
    for i in range(HALF_HEADS):
        hd = core * HALF_HEADS + i
        for way in range(2):
            own, far = states[way, hd].astype(F32), sib[way, i].astype(F32)
            s_even, s_odd = jnp.where(core == 0, own, far), jnp.where(core == 0, far, own)
            if way == 0:
                whole = s_odd + jnp.exp(log_total(odd, hd)) * s_even
            else:
                whole = s_even + jnp.exp(log_total(even, hd)) * s_odd
            whole = whole.astype(BF16)
            for quarter in range(4):
                totals[quarter, way, i] = whole[quarter]
    for d in (1, 2, 3):
        wires.send(("z", d), totals.at[turn_z[d]], z_in.at[here.z], here.at(z=turn_z[d]))
    z_in[here.z] = totals[here.z]
    for h in range(0, 6):
        local(h)
    for d in (1, 2, 3):
        wires.arrived(("z", d), z_in.at[turn_z[4 - d]])

    def chip_decay(y, z, hd):
        chip = (y * 4 + z) * 2
        return log_total(chip, hd) + log_total(chip + 1, hd)

    for i in range(HALF_HEADS):
        hd = core * HALF_HEADS + i
        for way in range(2):
            order = range(4) if way == 0 else range(3, -1, -1)
            acc = jnp.zeros((32, HD), F32)
            for z in order:
                acc = z_in[z, way, i].astype(F32) + jnp.exp(chip_decay(here.y, z, hd)) * acc
            y_in[here.y, way, i] = acc.astype(BF16)
    for d in (1, 2, 3):
        wires.send(("y", d), y_in.at[here.y], y_in.at[here.y], here.at(y=turn_y[d]))
    for h in range(6, HEADS):
        local(h)
    for d in (1, 2, 3):
        wires.arrived(("y", d), y_in.at[turn_y[4 - d]])

    for i in range(HALF_HEADS):
        hd = core * HALF_HEADS + i
        for way in range(2):
            acc = jnp.zeros((32, HD), F32)
            for y in (0, 1, 2) if way == 0 else (3, 2, 1):
                line = chip_decay(y, 0, hd)
                for z in (1, 2, 3):
                    line = line + chip_decay(y, z, hd)
                ahead = y < here.y if way == 0 else y > here.y
                acc = jnp.where(ahead, y_in[y, way, i].astype(F32) + jnp.exp(line) * acc, acc)
            order = range(4) if way == 0 else range(3, -1, -1)
            for z in order:
                results[z, way, i] = acc.astype(BF16)
                acc = z_in[z, way, i].astype(F32) + jnp.exp(chip_decay(here.y, z, hd)) * acc
    for d in (1, 2, 3):
        wires.send(("r", d), results.at[turn_z[d]], r_in.at[here.z], here.at(z=turn_z[d]))
    r_in[here.z] = results[here.z]
    for d in (1, 2, 3):
        wires.arrived(("r", d), r_in.at[turn_z[4 - d]])

    for i in range(HALF_HEADS):
        hd = core * HALF_HEADS + i
        for way in range(2):
            own, far = states[way, hd].astype(F32), sib[way, i].astype(F32)
            s_even, s_odd = jnp.where(core == 0, own, far), jnp.where(core == 0, far, own)
            enters = jnp.stack([r_in[quarter, way, i] for quarter in range(4)], axis=0).astype(F32)
            if way == 0:
                at_even = enters
                at_odd = s_even + jnp.exp(log_total(even, hd)) * enters
            else:
                at_odd = enters
                at_even = s_odd + jnp.exp(log_total(odd, hd)) * enters
            final[way, hd] = jnp.where(core == 0, at_even, at_odd).astype(BF16)
            for_sib[way, i] = jnp.where(core == 0, at_odd, at_even).astype(BF16)
    own_heads = pl.ds(core * HALF_HEADS, HALF_HEADS)
    wires.send("f", for_sib, final.at[:, own_heads], here.sibling())
    wires.arrived("f", final.at[:, pl.ds(other * HALF_HEADS, HALF_HEADS)])

    for h in range(HEADS):
        _, k, v, g = head(h)
        front, tail = columns(h)
        state_in, state_grad = final[0, h].reshape(HD, HD), final[1, h].reshape(HD, HD)
        at = slice(h * HD, (h + 1) * HD)
        dq_out[:, at] = (kept[0, h] + front * dot_nt(g, state_in)).astype(BF16)
        dk_out[:, at] = (kept[1, h] + tail * dot_nt(v, state_grad)).astype(BF16)
        dv_out[:, at] = (kept[2, h] + tail * dot(k, state_grad)).astype(BF16)
    wires.drain()


def in_vmem(count):
    return [pl.BlockSpec(memory_space=pltpu.VMEM)] * count


def in_hbm(count):
    return [pl.BlockSpec(memory_space=pl.ANY)] * count


def shape(dims, kind=BF16):
    return jax.ShapeDtypeStruct(dims, kind)


def moe_call(small, moe_input, out_grad, w_gate, w_up, w_down):
    sems = 80
    return pl.pallas_call(
        moe_kernel,
        out_shape=(
            shape((SLOTS, D)),
            shape((SLOTS, D)),
            shape((SLOTS, HID)),
            shape((SLOTS, HID)),
            shape((SLOTS, HID)),
            shape((ROWS, QUARTER)),
            shape((32, 16, ROWS), F32),
        ),
        in_specs=in_vmem(3) + in_hbm(3),
        out_specs=tuple(in_hbm(2) + in_vmem(5)),
        scratch_shapes=[
            pltpu.VMEM((D, HID), BF16),
            pltpu.VMEM((D, HID), BF16),
            pltpu.VMEM((HID, D), BF16),
            pltpu.VMEM((2, SLOTS, WIDE), BF16),
            pltpu.VMEM((2, 64, QUARTER + 384), BF16),
            pltpu.VMEM((64, QUARTER + 384), BF16),
            pltpu.VMEM((4, 16, 384), BF16),
            pltpu.VMEM((3, SLOTS, HID), F32),
            pltpu.VMEM((SLOTS, HID), BF16),
            pltpu.VMEM((SLOTS, HID), BF16),
            pltpu.VMEM((2, MAIN, SHARE), BF16),
            pltpu.VMEM((MAIN, SHARE), BF16),
            pltpu.VMEM((MAIN, 384), BF16),
            pltpu.VMEM((64, SHARE_CUT), BF16),
            pltpu.VMEM((64, SHARE - SHARE_CUT), BF16),
            pltpu.VMEM((64, SHARE), BF16),
            pltpu.VMEM((64, SHARE), BF16),
            pltpu.VMEM((64, SHARE), BF16),
            pltpu.VMEM((16, SHARE_CUT), BF16),
            pltpu.VMEM((16, SHARE - SHARE_CUT), BF16),
            pltpu.VMEM((16, SHARE), BF16),
            pltpu.VMEM((16, SHARE), BF16),
            pltpu.VMEM((16, SHARE), BF16),
            pltpu.VMEM((2, 64, 1152), BF16),
            pltpu.VMEM((32, 16, ROWS), F32),
            pltpu.SemaphoreType.DMA((sems,)),
            pltpu.SemaphoreType.DMA((sems,)),
            pltpu.SemaphoreType.DMA((5,)),
        ],
        compiler_params=pltpu.CompilerParams(
            collective_id=0, has_side_effects=True, vmem_limit_bytes=BIG
        ),
        name="routed_experts",
    )(small, moe_input, out_grad, w_gate, w_up, w_down)


def scan_call(small, decay, queries, keys, values, attn_grad):
    sems = 16
    half = (HALF_HEADS, 4, 32, HD)
    piece = (4, 2, HALF_HEADS, 32, HD)
    return pl.pallas_call(
        scan_kernel,
        out_shape=(shape((ROWS, QUARTER)),) * 3,
        in_specs=in_vmem(6),
        out_specs=tuple(in_vmem(3)),
        scratch_shapes=[
            pltpu.VMEM((2, HEADS, 4, 32, HD), BF16),
            pltpu.VMEM((2,) + half, BF16),
            pltpu.VMEM(piece, BF16),
            pltpu.VMEM(piece, BF16),
            pltpu.VMEM(piece, BF16),
            pltpu.VMEM(piece, BF16),
            pltpu.VMEM(piece, BF16),
            pltpu.VMEM((2,) + half, BF16),
            pltpu.VMEM((2, HEADS, 4, 32, HD), BF16),
            pltpu.VMEM((ROWS, ROWS), F32),
            pltpu.VMEM((3, HEADS, ROWS, HD), F32),
            pltpu.SemaphoreType.DMA((sems,)),
            pltpu.SemaphoreType.DMA((sems,)),
        ],
        compiler_params=pltpu.CompilerParams(
            collective_id=1, has_side_effects=True, vmem_limit_bytes=BIG
        ),
        name="state_scans",
    )(small, decay, queries, keys, values, attn_grad)


def on_device(
    queries, keys, values, log_decay, moe_input, out_grad, expert_ids, route_gates, w_gate, w_up, w_down
):
    small = jnp.concatenate(
        [
            jnp.pad(log_decay, ((0, 4), (0, 0))),
            expert_ids.T.astype(F32),
            route_gates.T,
            jnp.zeros((4, ROWS), F32),
        ],
        axis=0,
    )
    inputs, grads, hidden, gate_act, up_act, attn_grad, decay = moe_call(
        small, moe_input, out_grad, w_gate[0], w_up[0], w_down[0]
    )
    query_grad, key_grad, value_grad = scan_call(small, decay, queries, keys, values, attn_grad)
    gate_part = dot_tn(inputs, gate_act).astype(BF16)
    up_part = dot_tn(inputs, up_act).astype(BF16)
    down_part = dot_tn(hidden, grads).astype(BF16)
    return (query_grad, key_grad, value_grad, gate_part[None], up_part[None], down_part[None])


def solution(mesh):
    rows, heads = P("ctx", "exp"), P("exp", "ctx")
    columns, down = P("exp", None, "ctx"), P("exp", "ctx", None)
    return jax.shard_map(
        on_device,
        mesh=mesh,
        in_specs=(rows, rows, rows, heads, rows, rows, P("ctx", None), P("ctx", None), columns, columns, down),
        out_specs=(rows, rows, rows, columns, columns, down),
        check_vma=False,
    )
```

time: 500 us -> 129 us (0.26); the launches traced: 493 us -> 129 us
  waiting for transfers between devices: 222 us -> 0 us
  Pallas kernels: 0 us -> 111 us
  other arithmetic: 75.2 us -> 2.05 us
  blocking collectives: 65.3 us -> 0 us
  local copies, waits for them, and re-layouts: 60.3 us -> 2.34 us
  matrix products: 39.6 us -> 12.7 us
  between operations: 16 us -> 0.7 us
  starting transfers between devices: 13.8 us -> 0 us
    pallas_call x0 -> x2, Pallas kernels: none -> 111 us  [the longest x1 79.2 us: moe_call(): pl.pallas_call(moe_kernel, out_shape=(shape((SLOTS, D)), shape((SLOTS, D)...]
    unnamed x6 -> x0, waiting for transfers between devices: 104 us -> none
    all_gather x4 -> x0, waiting for transfers between devices: 84 us -> none  [the longest x1 45.4 us: on_device(): lax.all_gather(slot_inputs, 'ctx', axis=1, tiled=True)]
    unnamed x1 -> x0, blocking collectives: 65.3 us -> none
    add x31 -> x0, other arithmetic: 37.2 us -> none  [join_states(): later[0][:, None, None] * earlier[1] + later[1]]
    unnamed x2 -> x0, other arithmetic: 34.5 us -> none
    all_to_all x3 -> x0, waiting for transfers between devices: 33.8 us -> none  [the longest x1 30.9 us: on_device(): lax.all_to_all(spread[1], 'exp', split_axis=0, concat_axis=2, tiled=True)]
    dot_general x23 -> x3, matrix products: 39.6 us -> 12.7 us  [dot_tn(): lax.dot_general(a, b, (((0,), (0,)), ((), ())), preferred_element_type=F32)]
  transfers between devices with their start and end apart: 8 -> 0, of which waited for: 5 -> 0; matrix products, arithmetic and copies ran while one was open for 21% -> 0% of each run, Pallas kernels for 0% -> 0%
where the time goes in v1:
time: 129 us
  Pallas kernels  111 us (86%)
  matrix products  12.7 us (10%)
  local copies, waits for them, and re-layouts  2.34 us (2%)
  other arithmetic  2.05 us (2%)
    pallas_call x1, Pallas kernels, moe_call(): pl.pallas_call(moe_kernel, out_shape=(shape((SLOTS, D)), shape((SLOTS, D)...  79.2 us
    pallas_call x1, Pallas kernels, scan_call(): pl.pallas_call(scan_kernel, out_shape=(shape((ROWS, QUARTER)),) * 3, in_s...  32 us
    dot_general x3, matrix products, dot_tn(): lax.dot_general(a, b, (((0,), (0,)), ((), ())), preferred_element_type=F32)  12.7 us

profile of v1, /device:TPU:1, one launch (start us, length us, event | category | flops | bytes accessed | tf_op | source)
XLA Modules:
  0.0 129.0 jit_solution(15927998615847495950)
XLA Ops:
  0.6 0.1 pad.8.clone
  0.7 0.7 convert_bitcast_fusion
  1.4 1.4 %fusion.4.small_ref = f32[24,128]{1,0:T(8,128)} fusion(f32[12,128]{1,0:T(8,128)} %param.14, f32[2,128]{1,0:T(2,128)} %bitcast.21, f32[2,128]{1,0:T(2,128)S(1)} %convert_bitcast_fusion, f32[24]{0:T(128)S(1)} %pad.8.clone), kind=kLoop, calls=%fused_computation.8 | loop fusion | flops 15360 | bytes 20576 | tf_op jit(solution)/shard_map/concatenate | solution.py:686
  2.8 79.2 %routed_experts.1 = (bf16[288,6144]{1,0:T(8,128)(2,1)}, bf16[288,6144]{1,0:T(8,128)(2,1)}, bf16[288,256]{1,0:T(8,128)(2,1)}, bf16[288,256]{1,0:T(8,128)(2,1)}, b...) custom-call(f32[24,128]{1,0:T(8,128)} %fusion.4.small_ref, bf16[128,1536]{1,0:T(8,128)(2,1)} %moe_ref.1, ...), custom_call_target="tpu_custom_call" | custom-call | tf_op jit(solution)/shard_map/routed_experts/pallas_call | solution.py:602
  82.0 32.0 %state_scans.1 = (bf16[128,1536]{1,0:T(8,128)(2,1)}, bf16[128,1536]{1,0:T(8,128)(2,1)}, bf16[128,1536]{1,0:T(8,128)(2,1)}) custom-call(f32[24,128]{1,0:T(8,128)} %fusion.4.small_ref, f32[32,16,128]{2,1,0:T(8,128)} %get-tuple-element.16.decay_ref, bf16[128,1536]{1,0:T(8,128)(2,1)} %q_ref.1, bf16[128,1536]{1,0:T(8,128)(2,1)} %k_ref.1, ...), custom_call_target="tpu_custom_call" | custom-call | tf_op jit(solution)/shard_map/state_scans/pallas_call | solution.py:656
  114.0 0.0 copy-start.5
  114.0 0.0 copy-start.6
  114.0 5.7 %fusion = bf16[1,6144,256]{2,1,0:T(8,128)(2,1)} fusion(bf16[288,6144]{1,0:T(8,128)(2,1)} %get-tuple-element.21, bf16[288,256]{1,0:T(8,128)(2,1)} %get-tuple-element.22), kind=kOutput, calls=%fused_computation.3 | convolution fusion | flops 907542528 | bytes 6832128 | tf_op jit(solution)/shard_map/dot_general | solution.py:39
  119.7 0.0 copy-done.5
  119.7 0.0 copy-done.6
  119.7 0.0 copy-start
  119.7 0.0 copy-start.4
  119.7 3.5 %fusion.1 = bf16[1,6144,256]{2,1,0:T(8,128)(2,1)} fusion(bf16[288,6144]{1,0:T(8,128)(2,1)S(1)} %copy-done.5, bf16[288,256]{1,0:T(8,128)(2,1)S(1)} %copy-done.6), kind=kOutput, calls=%fused_computation.4 | convolution fusion | flops 907542528 | bytes 6832128 | tf_op jit(solution)/shard_map/dot_general | solution.py:39
  123.2 0.0 copy-done
  123.2 0.0 copy-done.4
  123.2 0.0 copy-start.3
  123.2 0.0 copy-start.2
  123.2 0.0 copy-start.1
  123.2 3.5 %fusion.2 = bf16[1,256,6144]{2,1,0:T(8,128)(2,1)} fusion(bf16[288,256]{1,0:T(8,128)(2,1)S(1)} %copy-done.4, bf16[288,6144]{1,0:T(8,128)(2,1)S(1)} %copy-done), kind=kOutput, calls=%fused_computation.5 | convolution fusion | flops 907542528 | bytes 6832128 | tf_op jit(solution)/shard_map/dot_general | solution.py:39
  126.7 0.0 copy-done.3
  126.7 0.7 copy.20
  127.5 0.0 copy-done.2
  127.5 0.7 copy.21
  128.2 0.0 copy-done.1
  128.2 0.7 copy.22
  (1 shorter events, 0.0 us)
Async XLA Ops:
  114.0 5.7 %copy-start.5 = (bf16[288,6144]{1,0:T(8,128)(2,1)S(1)}, bf16[288,6144]{1,0:T(8,128)(2,1)}, u32[]{:S(2)}) copy-start(bf16[288,6144]{1,0:T(8,128)(2,1)} %get-tuple-element.21) | copy-start | bytes 10616836
  114.0 5.7 %copy-start.6 = (bf16[288,256]{1,0:T(8,128)(2,1)S(1)}, bf16[288,256]{1,0:T(8,128)(2,1)}, u32[]{:S(2)}) copy-start(bf16[288,256]{1,0:T(8,128)(2,1)} %get-tuple-element.23) | copy-start | bytes 442372
  119.7 3.5 %copy-start = (bf16[288,6144]{1,0:T(8,128)(2,1)S(1)}, bf16[288,6144]{1,0:T(8,128)(2,1)}, u32[]{:S(2)}) copy-start(bf16[288,6144]{1,0:T(8,128)(2,1)} %get-tuple-element.25) | copy-start | bytes 10616836
  119.7 3.5 %copy-start.4 = (bf16[288,256]{1,0:T(8,128)(2,1)S(1)}, bf16[288,256]{1,0:T(8,128)(2,1)}, u32[]{:S(2)}) copy-start(bf16[288,256]{1,0:T(8,128)(2,1)} %get-tuple-element.24) | copy-start | bytes 442372
  123.2 3.5 %copy-start.3 = (bf16[128,1536]{1,0:T(8,128)(2,1)S(1)}, bf16[128,1536]{1,0:T(8,128)(2,1)}, u32[]{:S(2)}) copy-start(bf16[128,1536]{1,0:T(8,128)(2,1)} %get-tuple-element.32) | copy-start | bytes 1179652
  123.2 4.3 %copy-start.2 = (bf16[128,1536]{1,0:T(8,128)(2,1)S(1)}, bf16[128,1536]{1,0:T(8,128)(2,1)}, u32[]{:S(2)}) copy-start(bf16[128,1536]{1,0:T(8,128)(2,1)} %get-tuple-element.33) | copy-start | bytes 1179652
  123.2 5.0 %copy-start.1 = (bf16[128,1536]{1,0:T(8,128)(2,1)S(1)}, bf16[128,1536]{1,0:T(8,128)(2,1)}, u32[]{:S(2)}) copy-start(bf16[128,1536]{1,0:T(8,128)(2,1)} %get-tuple-element.34) | copy-start | bytes 1179652

commit v2 on v1

v2 whole, which is shorter than its diff:
```python
import jax
import jax.numpy as jnp
from jax import lax
from jax.experimental import pallas as pl
from jax.experimental.pallas import tpu as pltpu
from jax.sharding import PartitionSpec as P

MESH = pl.DeviceIdType.MESH
BF16 = jnp.bfloat16
F32 = jnp.float32

FLIGHT = 4
D = 6144
QUARTER = D // 4
HID = 256
HEADS = 12
HALF_HEADS = HEADS // 2
HD = 128
ROWS = 128
MAIN = 256
SLOTS = 288
PAIR = 2 * QUARTER + 384
PAIR_CUT = 1792
WIDE = 2 * PAIR
CHUNKS = (1536, 1920)
CHUNK_CUTS = (768, 1024)
SENDS = 91
RECEIVES = 133
BIG = 42 * 1024 * 1024


def dot(a, b):
    return lax.dot_general(a, b, (((1,), (0,)), ((), ())), preferred_element_type=F32)


def dot_nt(a, b):
    return lax.dot_general(a, b, (((1,), (1,)), ((), ())), preferred_element_type=F32)


def dot_tn(a, b):
    return lax.dot_general(a, b, (((0,), (0,)), ((), ())), preferred_element_type=F32)


def iota(shape, dim):
    return lax.broadcasted_iota(jnp.int32, shape, dim)


def aligned(value, by):
    return pl.multiple_of(value, by)


class Place:
    def __init__(self):
        ctx = lax.axis_index("ctx")
        self.x = lax.axis_index("exp")
        self.ctx = ctx
        self.core = lax.rem(ctx, 2)
        self.z = lax.rem(lax.div(ctx, 2), 4)
        self.y = lax.div(ctx, 8)
        self.chip = self.y * 4 + self.z

    def at(self, y=None, z=None, core=None, x=None):
        y = self.y if y is None else y
        z = self.z if z is None else z
        core = self.core if core is None else core
        x = self.x if x is None else x
        return (y * 8 + z * 2 + core, x)

    def sibling(self):
        return self.at(core=1 - self.core)


class Wires:
    def __init__(self, place, send_sems, recv_sems):
        self.place, self.send_sems, self.recv_sems = place, send_sems, recv_sems
        self.names, self.sent, self.most = {}, [], 0

    def slot(self, name):
        return self.names.setdefault(name, len(self.names))

    def send(self, name, src, dst, device):
        copy = pltpu.make_async_remote_copy(
            src_ref=src,
            dst_ref=dst,
            send_sem=self.send_sems.at[len(self.sent)],
            recv_sem=self.recv_sems.at[self.slot(name)],
            device_id=device,
            device_id_type=MESH,
        )
        copy.start()
        self.sent.append(copy)
        self.most = max(self.most, len(self.sent))

    def arrived(self, name, region):
        pltpu.make_async_remote_copy(
            src_ref=region,
            dst_ref=region,
            send_sem=self.send_sems.at[0],
            recv_sem=self.recv_sems.at[self.slot(name)],
            device_id=self.place.sibling(),
            device_id_type=MESH,
        ).wait_recv()

    def drain(self):
        for copy in self.sent:
            copy.wait_send()
        self.sent = []

    def check(self):
        assert self.most == SENDS and len(self.names) == RECEIVES, (self.most, len(self.names))


def greet(devices):
    for device in devices:
        pl.semaphore_signal(pltpu.get_barrier_semaphore(), inc=1, device_id=device, device_id_type=MESH)


def greeted(count):
    pl.semaphore_wait(pltpu.get_barrier_semaphore(), count)


def route_masks(ids, route_gates, place):
    wanted = iota((8, ROWS), 0)
    first = ids[0:1, :] == wanted
    second = ids[1:2, :] == wanted
    onehot = jnp.where(first | second, 1.0, 0.0)
    gates = jnp.where(first, route_gates[0:1, :], 0.0) + jnp.where(second, route_gates[1:2, :], 0.0)
    before = jnp.where(iota((ROWS, ROWS), 0) < iota((ROWS, ROWS), 1), 1.0, 0.0).astype(BF16)
    rank = dot(onehot.astype(BF16), before)
    rank = jnp.where(onehot > 0.5, rank, -1.0)

    def spread(a):
        return jnp.concatenate([jnp.broadcast_to(a[e : e + 1, :], (16, ROWS)) for e in range(FLIGHT)], axis=0)

    rank, gates = spread(rank), spread(gates)
    row = lax.rem(iota((64, ROWS), 0), 16)
    mine = lax.div(row, 8) == place.core
    slot = lax.rem(row, 8)
    main = jnp.where(mine & (rank == slot.astype(F32)), 1.0, 0.0)
    ninth = jnp.where(mine & (rank == 8.0), 1.0, 0.0)
    return main, ninth, slot, gates


def main_kernel(
    ids_hbm, route_gates_hbm, log_decay_hbm, moe_hbm, out_grad_hbm, q_hbm, k_hbm, v_hbm, wg_hbm, wu_hbm, wd_hbm,
    gate_out, up_out, down_out, dq, kept, state_out, tails,
    ids_ref, route_gates_ref, log_decay_ref,
    moe_ref, out_grad_ref, q_ref, k_ref, v_ref, wg, wu, wd, rows, stage, staged, ninth_in, acc, hidden, acts,
    part0, part1, theirs0, theirs1, fold,
    a0, b0, m0, p0, group0, landing0, a1, b1, m1, p1, group1, landing1,
    final0, final1, outgoing, back, decay, run, turned, scaled, attn,
    states, sib, totals, z_in, y_in, results, r_in, for_sib, final,
    send_sems, recv_sems, local_sems,
):
    here = Place()
    core, other = here.core, 1 - here.core
    wires = Wires(here, send_sems, recv_sems)
    def local_copy(src, dst, index):
        copy = pltpu.make_async_copy(src, dst, local_sems.at[index])
        copy.start()
        return copy

    across = [here.x, here.x + 1 - 2 * lax.rem(here.x, 2), lax.rem(here.x + 2, 4), 3 - here.x]
    turn_y = [lax.rem(here.y + d, 4) for d in range(4)]
    turn_z = [lax.rem(here.z + d, 4) for d in range(4)]
    greet(
        [here.sibling()]
        + [here.at(x=across[d]) for d in (1, 2, 3)]
        + [here.at(y=turn_y[d]) for d in (1, 2, 3)]
        + [here.at(z=turn_z[d]) for d in (1, 2, 3)]
    )
    tiny = [
        local_copy(log_decay_hbm, log_decay_ref, 0),
        local_copy(ids_hbm, ids_ref, 1),
        local_copy(route_gates_hbm, route_gates_ref, 2),
    ]
    early = [local_copy(moe_hbm, moe_ref, 3), local_copy(out_grad_hbm, out_grad_ref, 4)]
    soon = [local_copy(k_hbm, k_ref, 5), local_copy(q_hbm, q_ref, 6), local_copy(v_hbm, v_ref, 7)]
    loads = [local_copy(wg_hbm, wg, 8), local_copy(wu_hbm, wu, 9), local_copy(wd_hbm, wd, 10)]
    for load in tiny:
        load.wait()

    run[...] = jnp.zeros_like(run)
    run[0:HEADS, :] = log_decay_ref[...]
    log_decay = run[...]
    decay[here.ctx] = jnp.broadcast_to(jnp.sum(log_decay, axis=1, keepdims=True), (16, ROWS))

    main, ninth, slot, gates = route_masks(ids_ref[...], route_gates_ref[...], here)
    pick = main.astype(BF16)
    main_gate = jnp.sum(main * gates, axis=1, keepdims=True)
    ninth_gate = jnp.sum(ninth * gates, axis=1, keepdims=True)
    fold_at = lax.rem(here.x, 2) * 4
    for load in early:
        load.wait()
    picks = [jnp.where(slot == fold_at + b, ninth, 0.0).astype(BF16) for b in range(4)]
    for which, source in enumerate((moe_ref, out_grad_ref)):
        chosen = dot(pick, source[...])
        extra = dot(picks[0], source[:, 0:384])
        for b in range(1, 4):
            extra = extra + dot(picks[b], source[:, 384 * b : 384 * (b + 1)])
        if which:
            chosen, extra = chosen * main_gate, extra * ninth_gate
        stage[which, :, 0:QUARTER] = chosen.astype(BF16)
        stage[which, :, QUARTER:] = extra.astype(BF16)
    greeted(10)
    wires.send("s", stage.at[other], staged, here.sibling())
    wires.send("d", decay.at[here.ctx], decay.at[here.ctx], here.sibling())

    lane = iota((16, ROWS), 1)
    step = 1
    while step < ROWS:
        log_decay = log_decay + jnp.where(lane >= step, pltpu.roll(log_decay, step, 1), 0.0)
        step *= 2
    run[...] = log_decay
    turned[...] = jnp.concatenate([log_decay, jnp.zeros((ROWS - 16, ROWS), F32)], axis=0).T
    ends = jnp.concatenate(
        [jnp.broadcast_to(log_decay[:, ROWS - 1 :], (16, ROWS)), jnp.zeros((ROWS - 16, ROWS), F32)], axis=0
    ).T
    tails[...] = jnp.exp(ends - turned[...])

    wires.arrived("s", staged)
    stage[core] = (stage[core].astype(F32) + staged[...].astype(F32)).astype(BF16)

    mine = rows.at[core]
    own_rows = pl.ds(aligned(here.chip * 16, 16), 16)

    def quarter_at(x):
        return pl.ds(aligned(lax.div(x, 2) * PAIR + lax.rem(x, 2) * QUARTER, 128), QUARTER)

    for d in (1, 2, 3):
        to = pl.ds(aligned(across[d] * 16, 16), 16)
        wires.send(
            ("x", d), stage.at[core, to, 0:QUARTER], mine.at[own_rows, quarter_at(here.x)], here.at(x=across[d])
        )
        wires.send(("xr", d), stage.at[core, to, QUARTER:], ninth_in.at[here.x], here.at(x=across[d]))
    to = pl.ds(aligned(here.x * 16, 16), 16)
    rows[core, own_rows, quarter_at(here.x)] = stage[core, to, 0:QUARTER]
    ninth_in[here.x] = stage[core, to, QUARTER:]

    wires.arrived("d", decay.at[here.at(core=other)[0]])
    pair_of_blocks = decay.at[pl.ds(here.chip * 2, 2)]
    for d in (1, 2, 3):
        wires.send(("dz", d), pair_of_blocks, pair_of_blocks, here.at(z=turn_z[d]))

    def log_total(block, h):
        return decay[block, pl.ds(h, 1), :]

    def chip_decay(y, z, h):
        chip = (y * 4 + z) * 2
        return log_total(chip, h) + log_total(chip + 1, h)

    even, odd = here.chip * 2, here.chip * 2 + 1

    def scan(way, source):
        heads = [core * HALF_HEADS + i for i in range(HALF_HEADS)]
        order = range(4) if way == 0 else range(3, -1, -1)

        def own_states(half):
            for i in range(HALF_HEADS):
                h = half * HALF_HEADS + i
                at = pl.ds(aligned(h * HD, HD), HD)
                states[way, h] = dot_tn(scaled[way, :, at], source[:, at]).astype(BF16).reshape(4, 32, HD)

        def both_states(i):
            own, far = states[way, heads[i]].astype(F32), sib[way, i].astype(F32)
            return jnp.where(core == 0, own, far), jnp.where(core == 0, far, own)

        own_states(other)
        wires.send(("s", way), states.at[way, pl.ds(other * HALF_HEADS, HALF_HEADS)], sib.at[way], here.sibling())
        own_states(core)
        yield
        wires.arrived(("s", way), sib.at[way])
        for i, h in enumerate(heads):
            s_even, s_odd = both_states(i)
            if way == 0:
                whole = s_odd + jnp.exp(log_total(odd, h)) * s_even
            else:
                whole = s_even + jnp.exp(log_total(even, h)) * s_odd
            whole = whole.astype(BF16)
            for quarter in range(4):
                totals[way, quarter, i] = whole[quarter]
        for d in (1, 2, 3):
            wires.send(("z", way, d), totals.at[way, turn_z[d]], z_in.at[way, here.z], here.at(z=turn_z[d]))
        z_in[way, here.z] = totals[way, here.z]
        yield
        for d in (1, 2, 3):
            wires.arrived(("z", way, d), z_in.at[way, turn_z[4 - d]])
        for i, h in enumerate(heads):
            total = jnp.zeros((32, HD), F32)
            for z in order:
                total = z_in[way, z, i].astype(F32) + jnp.exp(chip_decay(here.y, z, h)) * total
            y_in[way, here.y, i] = total.astype(BF16)
        for d in (1, 2, 3):
            wires.send(("y", way, d), y_in.at[way, here.y], y_in.at[way, here.y], here.at(y=turn_y[d]))
        yield
        for d in (1, 2, 3):
            wires.arrived(("y", way, d), y_in.at[way, turn_y[4 - d]])
        for i, h in enumerate(heads):
            total = jnp.zeros((32, HD), F32)
            for y in (0, 1, 2) if way == 0 else (3, 2, 1):
                line = chip_decay(y, 0, h)
                for z in (1, 2, 3):
                    line = line + chip_decay(y, z, h)
                ahead = y < here.y if way == 0 else y > here.y
                total = jnp.where(ahead, y_in[way, y, i].astype(F32) + jnp.exp(line) * total, total)
            for z in order:
                results[way, z, i] = total.astype(BF16)
                total = z_in[way, z, i].astype(F32) + jnp.exp(chip_decay(here.y, z, h)) * total
        for d in (1, 2, 3):
            wires.send(("r", way, d), results.at[way, turn_z[d]], r_in.at[way, here.z], here.at(z=turn_z[d]))
        r_in[way, here.z] = results[way, here.z]
        yield
        for d in (1, 2, 3):
            wires.arrived(("r", way, d), r_in.at[way, turn_z[4 - d]])
        for i, h in enumerate(heads):
            s_even, s_odd = both_states(i)
            enters = jnp.stack([r_in[way, quarter, i] for quarter in range(4)], axis=0).astype(F32)
            if way == 0:
                at_even, at_odd = enters, s_even + jnp.exp(log_total(even, h)) * enters
            else:
                at_even, at_odd = s_odd + jnp.exp(log_total(odd, h)) * enters, enters
            for_sib[way, i] = jnp.where(core == 0, at_odd, at_even).astype(BF16)
            final[way, h] = jnp.where(core == 0, at_even, at_odd).astype(BF16)
        wires.send(("f", way), for_sib.at[way], final.at[way, pl.ds(core * HALF_HEADS, HALF_HEADS)], here.sibling())
        yield
        wires.arrived(("f", way), final.at[way, pl.ds(other * HALF_HEADS, HALF_HEADS)])
        yield

    for load in soon:
        load.wait()
    for h in range(HEADS):
        at = slice(h * HD, (h + 1) * HD)
        scaled[0, :, at] = (tails[:, h : h + 1] * k_ref[:, at].astype(F32)).astype(BF16)
        scaled[1, :, at] = (jnp.exp(turned[:, h : h + 1]) * q_ref[:, at].astype(F32)).astype(BF16)
    earlier = scan(0, v_ref)
    next(earlier)

    first = jnp.where(core == 0, here.z, here.y)
    second = jnp.where(core == 0, here.y, here.z)
    first_step, second_step = jnp.where(core == 0, 1, 4), jnp.where(core == 0, 4, 1)
    fs = [lax.rem(first + d, 4) for d in range(4)]
    ss = [lax.rem(second + d, 4) for d in range(4)]

    def on_first(value):
        return here.at(y=jnp.where(core == 0, here.y, value), z=jnp.where(core == 0, value, here.z))

    def on_second(value):
        return here.at(y=jnp.where(core == 0, value, here.y), z=jnp.where(core == 0, here.z, value))

    own_pair = lax.div(here.x, 2)
    pairs = (own_pair, 1 - own_pair)

    def enter(turn):
        for d in ((1,), (2, 3))[turn]:
            wires.arrived(("x", d), mine.at[own_rows, quarter_at(across[d])])
            wires.arrived(("xr", d), ninth_in.at[across[d]])
        p = pairs[turn]
        rows[core, own_rows, pl.ds(aligned(p * PAIR + 2 * QUARTER, 128), 384)] = (
            ninth_in[2 * p].astype(F32) + ninth_in[2 * p + 1].astype(F32)
        ).astype(BF16)

    def gather(turn):
        base = pairs[turn] * PAIR
        full = pl.ds(aligned(base, 128), PAIR)
        left = pl.ds(aligned(base, 128), PAIR_CUT)
        right = pl.ds(aligned(base + PAIR_CUT, 128), PAIR - PAIR_CUT)

        def tile(i, j, columns=full):
            at = (fs[i] * first_step + ss[j] * second_step) * 16
            return rows.at[core, pl.ds(aligned(at, 16), 16), columns]

        def send(name, region, device):
            wires.send((turn,) + name, region, region, device)

        def arrived(name, region):
            wires.arrived((turn,) + name, region)

        def share(i, j):
            send(("c", i, j), tile(i, j), here.sibling())

        def spread_second(i):
            send(("s+", i), tile(i, 0), on_second(ss[1]))
            send(("s-", i), tile(i, 0), on_second(ss[3]))
            share(i, 0)

        def pass_second(i):
            arrived(("s+", i), tile(i, 3))
            send(("s+l", i), tile(i, 3, left), on_second(ss[1]))
            share(i, 3)
            arrived(("s-", i), tile(i, 1))
            send(("s-r", i), tile(i, 1, right), on_second(ss[3]))
            share(i, 1)

        def end_second(i):
            arrived(("s+l", i), tile(i, 2, left))
            arrived(("s-r", i), tile(i, 2, right))
            share(i, 2)

        for d in (1, 3, 2):
            send(("f", d), tile(0, 0), on_first(fs[d]))
        spread_second(0)
        yield
        arrived(("f", 1), tile(3, 0))
        spread_second(3)
        arrived(("f", 3), tile(1, 0))
        spread_second(1)
        yield
        pass_second(0)
        yield
        arrived(("f", 2), tile(2, 0))
        spread_second(2)
        yield
        pass_second(3)
        yield
        pass_second(1)
        yield
        pass_second(2)
        yield
        end_second(0)
        yield
        end_second(3)
        yield
        end_second(1)
        yield
        end_second(2)
        yield
        for i in range(4):
            for j in range(4):
                at = (ss[i] * second_step + fs[j] * first_step) * 16
                arrived(("c", i, j), rows.at[other, pl.ds(aligned(at, 16), 16), full])
        yield

    enter(0)
    pull0, pull1 = gather(0), gather(1)
    next(pull0)
    enter(1)
    next(pull1)
    next(earlier)
    next(pull0)
    next(pull0)
    next(pull1)
    next(pull1)
    next(pull0)
    next(pull1)
    for d in (1, 2, 3):
        wires.arrived(("dz", d), decay.at[pl.ds((here.y * 4 + turn_z[4 - d]) * 2, 2)])
    line_of_blocks = decay.at[pl.ds(here.y * 8, 8)]
    for d in (1, 2, 3):
        wires.send(("dy", d), line_of_blocks, line_of_blocks, here.at(y=turn_y[d]))
    next(pull0)
    next(pull0)
    next(pull1)
    next(pull1)
    next(pull0)
    next(pull1)
    next(pull0)
    next(pull0)
    next(pull0)
    next(pull0)
    next(pull1)
    next(pull0)

    r0, r1 = iota((MAIN, MAIN), 0), iota((MAIN, MAIN), 1)

    def unfold(turn):
        chip_core, grp = lax.rem(r0, 32), lax.div(r0, 32)
        select = jnp.where(r1 == chip_core * 8 + grp, 1.0, 0.0).astype(BF16)
        base = pairs[turn] * PAIR
        for which in range(2):
            spread = dot(select, rows[which, 0:MAIN, pl.ds(aligned(base + 2 * QUARTER, 128), 384)]).astype(BF16)
            for g in range(8):
                at = pl.ds(aligned(base + g * 384, 128), 384)
                rows[which, MAIN:SLOTS, at] = spread[32 * g : 32 * (g + 1), :]

    def contract(turn, start, stop):
        def one(j, _):
            at = pl.ds(aligned(pairs[turn] * PAIR + j * 512, 128), 512)
            to = pl.ds(aligned(pairs[turn] * 2 * QUARTER + j * 512, 512), 512)
            inputs, grads = rows[0, :, at], rows[1, :, at]
            acc[0] += dot(inputs, wg[to, :])
            acc[1] += dot(inputs, wu[to, :])
            acc[2] += dot_nt(grads, wd[:, to])
            return 0

        lax.fori_loop(start, stop, one, 0)

    def weight_grads(start, stop):
        for i in range(start, stop):
            at = slice(1024 * i + 384 * (i // 3), 1024 * (i + 1) + 384 * (i // 3))
            to = slice(1024 * i, 1024 * (i + 1))
            both = dot_tn(rows[0, :, at], acts[...])
            gate_out[to, :] = both[:, 0:HID].astype(BF16)
            up_out[to, :] = both[:, HID:].astype(BF16)
            down_out[:, to] = dot_tn(hidden[...], rows[1, :, at]).astype(BF16)

    for load in loads:
        load.wait()
    acc[...] = jnp.zeros_like(acc)
    unfold(0)
    contract(0, 0, 2)
    next(pull1)
    contract(0, 2, 4)
    next(pull1)
    contract(0, 4, 6)
    next(pull1)
    for d in (1, 2, 3):
        wires.arrived(("dy", d), decay.at[pl.ds(turn_y[4 - d] * 8, 8)])
    next(earlier)
    next(pull1)
    unfold(1)
    contract(1, 0, 6)
    wires.drain()
    gate_pre, up_pre, hidden_grad = acc[0], acc[1], acc[2]
    sig = jax.nn.sigmoid(gate_pre)
    active = gate_pre * sig
    hidden[...] = (active * up_pre).astype(BF16)
    acts[:, 0:HID] = (hidden_grad * up_pre * sig * (1.0 + gate_pre * (1.0 - sig))).astype(BF16)
    acts[:, HID:] = (hidden_grad * active).astype(BF16)

    parts, theirs = (part0, part1), (theirs0, theirs1)

    def slot_part(which, owner, chunk):
        y_step, z_step = jnp.where(owner == 0, 4, 1), jnp.where(owner == 0, 1, 4)
        part = parts[chunk]

        def one(j, _):
            q = 2 * chunk + j
            at = pl.ds(aligned(q * QUARTER + owner * 768, 768), 768)
            piece = dot_nt(acts[:, 0:HID], wg[at, :]) + dot_nt(acts[:, HID:], wu[at, :])
            piece = piece.astype(BF16)
            columns = pl.ds(aligned(j * 768, 768), 768)
            for k in range(16):
                to = ((k // 4) * y_step + (k % 4) * z_step) * 16
                part[which, pl.ds(aligned(to, 16), 16), columns] = piece[16 * k : 16 * (k + 1), :]
            for b in range(2):
                fold[which, pl.ds(aligned((q * 2 + b) * 32, 32), 32), :] = piece[MAIN:, 384 * b : 384 * (b + 1)]
            return 0

        lax.fori_loop(0, 2, one, 0)
        if chunk:
            position, inside = lax.div(r0, 16), lax.rem(r0, 16)
            chip = jnp.where(owner == 0, position, lax.rem(position, 4) * 4 + lax.div(position, 4))
            source = lax.rem(inside, 8) * 32 + chip * 2 + lax.div(inside, 8)
            refold = jnp.where(r1 == source, 1.0, 0.0).astype(BF16)
            part[which, :, 1536:] = dot(refold, fold[which]).astype(BF16)

    def join(chunk):
        wires.arrived(("p", chunk), theirs[chunk])
        part, far = parts[chunk], theirs[chunk]

        def one(j, _):
            at = pl.ds(aligned(j * 16, 16), 16)
            part[0, at, :] = (part[0, at, :].astype(F32) + far[at, :].astype(F32)).astype(BF16)
            return 0

        lax.fori_loop(0, 16, one, 0)

    def ring_sum(tag, buffer, height, cut, places, device, in_a, in_b, in_m, in_p, result):
        cl, cr = pl.ds(0, cut), pl.ds(cut, in_m.shape[1] - cut)

        def block(i, columns):
            return buffer.at[pl.ds(aligned(places[i] * height, height), height), columns]

        def add_into(i, columns, arrived_ref):
            at = pl.ds(aligned(places[i] * height, height), height)
            buffer[at, columns] = (buffer[at, columns].astype(F32) + arrived_ref[...].astype(F32)).astype(BF16)

        up, down = device(places[1]), device(places[3])
        wires.send((tag, "a"), block(2, cl), in_a, up)
        wires.send((tag, "b"), block(2, cr), in_b, down)
        wires.send((tag, "mr"), block(1, cr), in_m.at[:, cr], up)
        wires.send((tag, "pl"), block(3, cl), in_p.at[:, cl], down)
        yield
        wires.arrived((tag, "a"), in_a)
        add_into(1, cl, in_a)
        wires.send((tag, "ml"), block(1, cl), in_m.at[:, cl], up)
        wires.arrived((tag, "b"), in_b)
        add_into(3, cr, in_b)
        wires.send((tag, "pr"), block(3, cr), in_p.at[:, cr], down)
        yield
        wires.arrived((tag, "mr"), in_m.at[:, cr])
        wires.arrived((tag, "pl"), in_p.at[:, cl])
        wires.arrived((tag, "ml"), in_m.at[:, cl])
        wires.arrived((tag, "pr"), in_p.at[:, cr])
        at = pl.ds(aligned(places[0] * height, height), height)
        result[...] = (buffer[at, :].astype(F32) + in_m[...].astype(F32) + in_p[...].astype(F32)).astype(BF16)
        yield

    def direct_sum(tag, buffer, places, device, landing, result):
        def block(i):
            return pl.ds(aligned(places[i] * 16, 16), 16)

        for d in (2, 1, 3):
            wires.send((tag, d), buffer.at[block(d), :], landing.at[d], device(places[d]))
        yield
        total = buffer[block(0), :].astype(F32)
        for d in (1, 3, 2):
            wires.arrived((tag, d), landing.at[d])
            total = total + landing[d].astype(F32)
        result[...] = total.astype(BF16)
        yield

    far0 = ring_sum("r0", part0.at[0], 64, CHUNK_CUTS[0], ss, on_second, a0, b0, m0, p0, group0)
    far1 = ring_sum("r1", part1.at[0], 64, CHUNK_CUTS[1], ss, on_second, a1, b1, m1, p1, group1)
    near0 = direct_sum("n0", group0, fs, on_first, landing0, final0)
    near1 = direct_sum("n1", group1, fs, on_first, landing1, final1)
    slot_part(1, other, 0)
    wires.send(("p", 0), part0.at[1], theirs0, here.sibling())
    slot_part(0, core, 0)
    slot_part(1, other, 1)
    wires.send(("p", 1), part1.at[1], theirs1, here.sibling())
    join(0)
    next(far0)
    slot_part(0, core, 1)
    join(1)
    next(far1)
    next(far0)
    next(far1)
    next(far0)
    next(near0)
    next(far1)
    next(near1)
    next(near0)
    next(near1)

    own_back = pl.ds(aligned(here.x * 16, 16), 16)
    back_main = [final0.at[:, 0:768], final0.at[:, 768:1536], final1.at[:, 0:768], final1.at[:, 768:1536]]
    for q in range(4):
        outgoing[16 * q : 16 * (q + 1), :] = back_main[q][...]
    for d in (1, 2, 3):
        source = outgoing.at[pl.ds(aligned(across[d] * 16, 16), 16), :]
        wires.send(("b", d), source, back.at[core, own_back, 0:768], here.at(x=across[d]))
        wires.send(("br", d), final1.at[:, 1536:], back.at[core, own_back, 768:], here.at(x=across[d]))
    back[core, own_back, 0:768] = outgoing[own_back, :]
    back[core, own_back, 768:] = final1[:, 1536:]
    next(earlier)
    weight_grads(0, 2)
    for d in (1, 2, 3):
        source = pl.ds(aligned(across[d] * 16, 16), 16)
        wires.arrived(("b", d), back.at[core, source, 0:768])
        wires.arrived(("br", d), back.at[core, source, 768:])
    wires.send("bc", back.at[core], back.at[core], here.sibling())
    weight_grads(2, 3)
    wires.arrived("bc", back.at[other])

    for b in range(2):
        chosen = jnp.where(slot == 2 * here.x + b, ninth, 0.0)
        pick_back = jnp.concatenate([main, chosen], axis=0).astype(BF16)
        for h in range(2):
            at = h * 768 + b * 384
            source = jnp.concatenate([back[h, :, 384 * b : 384 * (b + 1)], back[h, :, 768:]], axis=0)
            attn[:, at : at + 384] = (
                out_grad_ref[:, at : at + 384].astype(F32) + dot_tn(pick_back, source)
            ).astype(BF16)

    later = scan(1, attn)
    next(later)
    next(earlier)
    next(later)
    next(earlier)

    lower = iota((ROWS, ROWS), 0) >= iota((ROWS, ROWS), 1)

    def within(h):
        at = slice(h * HD, (h + 1) * HD)
        q, k, v, g = q_ref[:, at], k_ref[:, at], v_ref[:, at], attn[:, at]
        front = turned[:, h : h + 1]
        spread = front - run[h : h + 1, :]
        w = jnp.where(lower, jnp.exp(jnp.where(lower, spread, 0.0)), 0.0)
        mixed = (dot_nt(g, v) * w).astype(BF16)
        scores = (dot_nt(q, k) * w).astype(BF16)
        state_in = final[0, h].reshape(HD, HD)
        dq[:, at] = (dot(mixed, k) + jnp.exp(front) * dot_nt(g, state_in)).astype(BF16)
        kept[0, :, at] = dot_tn(mixed, q)
        kept[1, :, at] = dot_tn(scores, g)

    for h in range(0, 6):
        within(h)
    next(later)
    for h in range(6, HEADS):
        within(h)
    next(later)
    weight_grads(3, 6)
    next(later)
    next(later)
    state_out[...] = final[1]
    wires.drain()
    wires.check()


def last_kernel(
    gate_ref, up_ref, down_ref, dq_ref, kept_ref, state_ref, tail_ref, k_hbm, v_hbm,
    gate_hbm, up_hbm, down_hbm, dq_out, dk_out, dv_out,
    k_ref, v_ref, dk_ref, dv_ref, sems,
):
    copies = []

    def start(src, dst):
        copy = pltpu.make_async_copy(src, dst, sems.at[len(copies)])
        copy.start()
        copies.append(copy)
        return copy

    loads = [start(k_hbm, k_ref), start(v_hbm, v_ref)]
    stores = [
        start(src, dst)
        for src, dst in ((gate_ref, gate_hbm), (up_ref, up_hbm), (down_ref, down_hbm), (dq_ref, dq_out))
    ]
    for load in loads:
        load.wait()
    for h in range(HEADS):
        at = slice(h * HD, (h + 1) * HD)
        tail, state = tail_ref[:, h : h + 1], state_ref[h].reshape(HD, HD)
        dk_ref[:, at] = (kept_ref[0, :, at] + tail * dot_nt(v_ref[:, at], state)).astype(BF16)
        dv_ref[:, at] = (kept_ref[1, :, at] + tail * dot(k_ref[:, at], state)).astype(BF16)
    stores += [start(dk_ref, dk_out), start(dv_ref, dv_out)]
    for store in stores:
        store.wait()


def in_vmem(count):
    return [pl.BlockSpec(memory_space=pltpu.VMEM)] * count


def in_hbm(count):
    return [pl.BlockSpec(memory_space=pl.ANY)] * count


def shape(dims, kind=BF16):
    return jax.ShapeDtypeStruct(dims, kind)


def main_call(ids, route_gates, log_decay, moe_input, out_grad, queries, keys, values, w_gate, w_up, w_down):
    half = (2, HALF_HEADS, 4, 32, HD)
    piece = (2, 4, HALF_HEADS, 32, HD)
    wide = (2, HEADS, 4, 32, HD)

    def ring(width, cut):
        return [(64, cut), (64, width - cut), (64, width), (64, width), (64, width), (4, 16, width)]

    bf16_scratch = (
        [(ROWS, QUARTER)] * 5
        + [(D, HID), (D, HID), (HID, D), (2, SLOTS, WIDE), (2, 64, QUARTER + 384), (64, QUARTER + 384), (4, 16, 384)],
        [(SLOTS, HID), (SLOTS, 2 * HID)]
        + [(2, MAIN, CHUNKS[0]), (2, MAIN, CHUNKS[1]), (MAIN, CHUNKS[0]), (MAIN, CHUNKS[1]), (2, MAIN, 384)]
        + ring(CHUNKS[0], CHUNK_CUTS[0])
        + ring(CHUNKS[1], CHUNK_CUTS[1])
        + [(16, CHUNKS[0]), (16, CHUNKS[1]), (64, 768), (2, 64, 1152)],
        [(2, ROWS, QUARTER), (ROWS, QUARTER), wide, half, piece, piece, piece, piece, piece, half, wide],
    )
    f32_scratch = (
        [(3, SLOTS, HID)],
        [(32, 16, ROWS), (16, ROWS), (ROWS, ROWS)],
        [],
    )
    scratch = [pltpu.VMEM((2, ROWS), jnp.int32), pltpu.VMEM((2, ROWS), F32), pltpu.VMEM((HEADS, ROWS), F32)]
    for narrow, broad in zip(bf16_scratch, f32_scratch):
        scratch += [pltpu.VMEM(dims, BF16) for dims in narrow]
        scratch += [pltpu.VMEM(dims, F32) for dims in broad]
    return pl.pallas_call(
        main_kernel,
        out_shape=(
            pltpu.VMEM((D, HID), BF16),
            pltpu.VMEM((D, HID), BF16),
            pltpu.VMEM((HID, D), BF16),
            pltpu.VMEM((ROWS, QUARTER), BF16),
            pltpu.VMEM((2, ROWS, QUARTER), F32),
            pltpu.VMEM((HEADS, 4, 32, HD), BF16),
            pltpu.VMEM((ROWS, ROWS), F32),
        ),
        in_specs=[pl.BlockSpec(memory_space=pltpu.HBM)] * 11,
        out_specs=tuple(in_vmem(7)),
        scratch_shapes=scratch
        + [
            pltpu.SemaphoreType.DMA((SENDS,)),
            pltpu.SemaphoreType.DMA((RECEIVES,)),
            pltpu.SemaphoreType.DMA((11,)),
        ],
        compiler_params=pltpu.CompilerParams(collective_id=0, has_side_effects=True, vmem_limit_bytes=BIG),
        name="routed_experts_and_scans",
    )(
        *(
            pltpu.with_memory_space_constraint(a, pltpu.HBM)
            for a in (
                ids, route_gates, log_decay, moe_input, out_grad, queries, keys, values, w_gate, w_up, w_down
            )
        )
    )


def last_call(gate_grad, up_grad, down_grad, dq, kept, state, tails, keys, values):
    held = (gate_grad, up_grad, down_grad, dq, kept, state, tails)
    outputs = [(D, HID), (D, HID), (HID, D), (ROWS, QUARTER), (ROWS, QUARTER), (ROWS, QUARTER)]
    return pl.pallas_call(
        last_kernel,
        out_shape=tuple(shape(dims) for dims in outputs),
        in_specs=in_vmem(7) + [pl.BlockSpec(memory_space=pltpu.HBM)] * 2,
        out_specs=tuple(in_hbm(len(outputs))),
        scratch_shapes=[pltpu.VMEM((ROWS, QUARTER), BF16)] * 4 + [pltpu.SemaphoreType.DMA((8,))],
        compiler_params=pltpu.CompilerParams(vmem_limit_bytes=16 * 1024 * 1024),
        name="outputs",
    )(*(pltpu.with_memory_space_constraint(a, pltpu.VMEM) for a in held), keys, values)


def on_device(
    queries, keys, values, log_decay, moe_input, out_grad, expert_ids, route_gates, w_gate, w_up, w_down
):
    held = main_call(
        expert_ids.T, route_gates.T, log_decay, moe_input, out_grad, queries, keys, values, w_gate[0], w_up[0], w_down[0]
    )
    gate_part, up_part, down_part, query_grad, key_grad, value_grad = last_call(*held, keys, values)
    return (query_grad, key_grad, value_grad, gate_part[None], up_part[None], down_part[None])


def solution(mesh):
    rows, heads = P("ctx", "exp"), P("exp", "ctx")
    columns, down = P("exp", None, "ctx"), P("exp", "ctx", None)
    return jax.shard_map(
        on_device,
        mesh=mesh,
        in_specs=(rows, rows, rows, heads, rows, rows, P("ctx", None), P("ctx", None), columns, columns, down),
        out_specs=(rows, rows, rows, columns, columns, down),
        check_vma=False,
    )
```

time: 129 us -> 93.9 us (0.73)
  Pallas kernels: 111 us -> 93 us
  matrix products: 12.7 us -> 0 us
  local copies, waits for them, and re-layouts: 2.34 us -> 0.01 us
  other arithmetic: 2.05 us -> 0 us
    pallas_call x2, Pallas kernels: 111 us -> 93 us  [the longest x1 88.5 us: main_call(): pl.pallas_call(main_kernel, out_shape=(pltpu.VMEM((D, HID), BF16), pltpu....]
    dot_general x3 -> x0, matrix products: 12.7 us -> none  [dot_tn(): lax.dot_general(a, b, (((0,), (0,)), ((), ())), preferred_element_type=F32)]
    unnamed x17 -> x4, local copies, waits for them, and re-layouts: 2.27 us -> 0.01 us
    concatenate x1 -> x0, other arithmetic: 1.37 us -> none  [on_device(): jnp.concatenate([jnp.pad(log_decay, ((0, 4), (0, 0))), expert_ids.T.astyp...]
where the time goes in v2:
time: 93.9 us; the launch traced here: 93.8 us
  Pallas kernels  93 us (99%)
    pallas_call x1, Pallas kernels, main_call(): pl.pallas_call(main_kernel, out_shape=(pltpu.VMEM((D, HID), BF16), pltpu....  88.5 us
    pallas_call x1, Pallas kernels, last_call(): pl.pallas_call(last_kernel, out_shape=tuple((shape(dims) for dims in outp...  4.44 us

profile of v2, /device:TPU:1, one launch (start us, length us, event | category | flops | bytes accessed | tf_op | source)
XLA Modules:
  0.0 93.8 jit_solution(12712105295043814753)
XLA Ops:
  0.6 0.0 copy-start
  0.6 0.0 copy-start.1
  0.7 88.5 %routed_experts_and_scans.1 = (bf16[6144,256]{1,0:T(8,128)(2,1)S(1)}, bf16[6144,256]{1,0:T(8,128)(2,1)S(1)}, bf16[256,6144]{1,0:T(8,128)(2,1)S(1)}, bf16[128,153...) custom-call(s32[2,128]{1,0:T(2,128)} %bitcast.11, ...), custom_call_target="tpu_custom_call" | custom-call | tf_op jit(solution)/shard_map/routed_experts_and_scans/pallas_call | solution.py:760
  89.2 0.0 copy-done
  89.2 0.0 copy-done.1
  89.2 4.4 %outputs.1 = (bf16[6144,256]{1,0:T(8,128)(2,1)}, bf16[6144,256]{1,0:T(8,128)(2,1)}, bf16[256,6144]{1,0:T(8,128)(2,1)}, bf16[128,1536]{1,0:T(8,128)(2,1)}, bf16[1...) custom-call(bf16[6144,256]{1,0:T(8,128)(2,1)S(1)} %get-tuple-element.19.gate_ref, ...), custom_call_target="tpu_custom_call" | custom-call | tf_op jit(solution)/shard_map/outputs/pallas_call | solution.py:794
Async XLA Ops:
  0.6 88.5 %copy-start = (bf16[128,1536]{1,0:T(8,128)(2,1)S(1)}, bf16[128,1536]{1,0:T(8,128)(2,1)}, u32[]{:S(2)}) copy-start(bf16[128,1536]{1,0:T(8,128)(2,1)} %k_hbm.3) | copy-start | bytes 1179652
  0.6 88.5 %copy-start.1 = (bf16[128,1536]{1,0:T(8,128)(2,1)S(1)}, bf16[128,1536]{1,0:T(8,128)(2,1)}, u32[]{:S(2)}) copy-start(bf16[128,1536]{1,0:T(8,128)(2,1)} %v_hbm.3) | copy-start | bytes 1179652

commit v3 on v2

--- a/solution.py
+++ b/solution.py
@@ -22,10 +22,11 @@
 PAIR = 2 * QUARTER + 384
 PAIR_CUT = 1792
 WIDE = 2 * PAIR
-CHUNKS = (1536, 1920)
-CHUNK_CUTS = (768, 1024)
-SENDS = 91
-RECEIVES = 133
+QUARTERS = ((0,), (1, 2), (3,))
+CHUNKS = (768, 1536, 1152)
+CHUNK_CUTS = (384, 768, 640)
+SENDS = 81
+RECEIVES = 182
 BIG = 42 * 1024 * 1024
 
 
@@ -73,23 +74,25 @@
 class Wires:
     def __init__(self, place, send_sems, recv_sems):
         self.place, self.send_sems, self.recv_sems = place, send_sems, recv_sems
-        self.names, self.sent, self.most = {}, [], 0
+        self.names, self.sent, self.free, self.most = {}, [], [], 0
 
     def slot(self, name):
         return self.names.setdefault(name, len(self.names))
 
     def send(self, name, src, dst, device):
+        if not self.free:
+            self.free, self.most = [self.most], self.most + 1
+        semaphore = self.free.pop()
         copy = pltpu.make_async_remote_copy(
             src_ref=src,
             dst_ref=dst,
-            send_sem=self.send_sems.at[len(self.sent)],
+            send_sem=self.send_sems.at[semaphore],
             recv_sem=self.recv_sems.at[self.slot(name)],
             device_id=device,
             device_id_type=MESH,
         )
         copy.start()
-        self.sent.append(copy)
-        self.most = max(self.most, len(self.sent))
+        self.sent.append((copy, semaphore))
 
     def arrived(self, name, region):
         pltpu.make_async_remote_copy(
@@ -101,10 +104,12 @@
             device_id_type=MESH,
         ).wait_recv()
 
-    def drain(self):
-        for copy in self.sent:
+    def drain(self, count=None):
+        count = len(self.sent) if count is None else count
+        for copy, semaphore in self.sent[:count]:
             copy.wait_send()
-        self.sent = []
+            self.free.append(semaphore)
+        self.sent = self.sent[count:]
 
     def check(self):
         assert self.most == SENDS and len(self.names) == RECEIVES, (self.most, len(self.names))
@@ -145,13 +150,16 @@
     ids_hbm, route_gates_hbm, log_decay_hbm, moe_hbm, out_grad_hbm, q_hbm, k_hbm, v_hbm, wg_hbm, wu_hbm, wd_hbm,
     gate_out, up_out, down_out, dq, kept, state_out, tails,
     ids_ref, route_gates_ref, log_decay_ref,
-    moe_ref, out_grad_ref, q_ref, k_ref, v_ref, wg, wu, wd, rows, stage, staged, ninth_in, acc, hidden, acts,
-    part0, part1, theirs0, theirs1, fold,
-    a0, b0, m0, p0, group0, landing0, a1, b1, m1, p1, group1, landing1,
-    final0, final1, outgoing, back, decay, run, turned, scaled, attn,
-    states, sib, totals, z_in, y_in, results, r_in, for_sib, final,
-    send_sems, recv_sems, local_sems,
+    moe_ref, out_grad_ref, q_ref, k_ref, v_ref, wgu, wd, rows, stage, staged, ninth_in, acc, acc_down, hidden, acts,
+    fold,
+    outgoing, back, decay, run, turned, scaled, attn,
+    states, sib, totals, t_in, results, r_in, for_sib, final,
+    *rest,
 ):
+    send_sems, recv_sems, local_sems = rest[-3:]
+    parts, theirs, in_as, in_bs, in_ms, in_ps, groups, landings, sums = (
+        rest[i : len(rest) - 3 : 9] for i in range(9)
+    )
     here = Place()
     core, other = here.core, 1 - here.core
     wires = Wires(here, send_sems, recv_sems)
@@ -163,20 +171,23 @@
     across = [here.x, here.x + 1 - 2 * lax.rem(here.x, 2), lax.rem(here.x + 2, 4), 3 - here.x]
     turn_y = [lax.rem(here.y + d, 4) for d in range(4)]
     turn_z = [lax.rem(here.z + d, 4) for d in range(4)]
-    greet(
-        [here.sibling()]
-        + [here.at(x=across[d]) for d in (1, 2, 3)]
-        + [here.at(y=turn_y[d]) for d in (1, 2, 3)]
-        + [here.at(z=turn_z[d]) for d in (1, 2, 3)]
-    )
     tiny = [
         local_copy(log_decay_hbm, log_decay_ref, 0),
         local_copy(ids_hbm, ids_ref, 1),
         local_copy(route_gates_hbm, route_gates_ref, 2),
     ]
     early = [local_copy(moe_hbm, moe_ref, 3), local_copy(out_grad_hbm, out_grad_ref, 4)]
+    greet(
+        [here.sibling()]
+        + [here.at(x=across[d]) for d in (1, 2, 3)]
+        + [here.at(y=turn_y[dy], z=turn_z[dz]) for dy in range(4) for dz in range(4) if dy or dz]
+    )
     soon = [local_copy(k_hbm, k_ref, 5), local_copy(q_hbm, q_ref, 6), local_copy(v_hbm, v_ref, 7)]
-    loads = [local_copy(wg_hbm, wg, 8), local_copy(wu_hbm, wu, 9), local_copy(wd_hbm, wd, 10)]
+    loads = [
+        local_copy(wg_hbm, wgu.at[:, 0:HID], 8),
+        local_copy(wu_hbm, wgu.at[:, HID:], 9),
+        local_copy(wd_hbm, wd, 10),
+    ]
     for load in tiny:
         load.wait()
 
@@ -202,7 +213,7 @@
             chosen, extra = chosen * main_gate, extra * ninth_gate
         stage[which, :, 0:QUARTER] = chosen.astype(BF16)
         stage[which, :, QUARTER:] = extra.astype(BF16)
-    greeted(10)
+    greeted(19)
     wires.send("s", stage.at[other], staged, here.sibling())
     wires.send("d", decay.at[here.ctx], decay.at[here.ctx], here.sibling())
 
@@ -227,12 +238,15 @@
     def quarter_at(x):
         return pl.ds(aligned(lax.div(x, 2) * PAIR + lax.rem(x, 2) * QUARTER, 128), QUARTER)
 
-    for d in (1, 2, 3):
+    def to_owner(d):
         to = pl.ds(aligned(across[d] * 16, 16), 16)
         wires.send(
             ("x", d), stage.at[core, to, 0:QUARTER], mine.at[own_rows, quarter_at(here.x)], here.at(x=across[d])
         )
         wires.send(("xr", d), stage.at[core, to, QUARTER:], ninth_in.at[here.x], here.at(x=across[d]))
+
+    to_owner(1)
+    to_owner(3)
     to = pl.ds(aligned(here.x * 16, 16), 16)
     rows[core, own_rows, quarter_at(here.x)] = stage[core, to, 0:QUARTER]
     ninth_in[here.x] = stage[core, to, QUARTER:]
@@ -245,21 +259,22 @@
     def log_total(block, h):
         return decay[block, pl.ds(h, 1), :]
 
-    def chip_decay(y, z, h):
-        chip = (y * 4 + z) * 2
-        return log_total(chip, h) + log_total(chip + 1, h)
-
     even, odd = here.chip * 2, here.chip * 2 + 1
+
+    apart = [(dy, dz) for dy in (2, 1, 3, 0) for dz in (2, 1, 3, 0) if dy or dz]
+
+    def chip_at(dy, dz):
+        return turn_y[dy % 4] * 4 + turn_z[dz % 4]
 
     def scan(way, source):
         heads = [core * HALF_HEADS + i for i in range(HALF_HEADS)]
-        order = range(4) if way == 0 else range(3, -1, -1)
+        order = range(16) if way == 0 else range(15, -1, -1)
 
         def own_states(half):
             for i in range(HALF_HEADS):
                 h = half * HALF_HEADS + i
                 at = pl.ds(aligned(h * HD, HD), HD)
-                states[way, h] = dot_tn(scaled[way, :, at], source[:, at]).astype(BF16).reshape(4, 32, HD)
+                states[way, h] = dot_tn(scaled[way, :, at], source[:, at]).astype(BF16).reshape(8, 16, HD)
 
         def both_states(i):
             own, far = states[way, heads[i]].astype(F32), sib[way, i].astype(F32)
@@ -277,44 +292,40 @@
             else:
                 whole = s_even + jnp.exp(log_total(even, h)) * s_odd
             whole = whole.astype(BF16)
-            for quarter in range(4):
-                totals[way, quarter, i] = whole[quarter]
-        for d in (1, 2, 3):
-            wires.send(("z", way, d), totals.at[way, turn_z[d]], z_in.at[way, here.z], here.at(z=turn_z[d]))
-        z_in[way, here.z] = totals[way, here.z]
-        yield
-        for d in (1, 2, 3):
-            wires.arrived(("z", way, d), z_in.at[way, turn_z[4 - d]])
-        for i, h in enumerate(heads):
-            total = jnp.zeros((32, HD), F32)
-            for z in order:
-                total = z_in[way, z, i].astype(F32) + jnp.exp(chip_decay(here.y, z, h)) * total
-            y_in[way, here.y, i] = total.astype(BF16)
-        for d in (1, 2, 3):
-            wires.send(("y", way, d), y_in.at[way, here.y], y_in.at[way, here.y], here.at(y=turn_y[d]))
-        yield
-        for d in (1, 2, 3):
-            wires.arrived(("y", way, d), y_in.at[way, turn_y[4 - d]])
-        for i, h in enumerate(heads):
-            total = jnp.zeros((32, HD), F32)
-            for y in (0, 1, 2) if way == 0 else (3, 2, 1):
-                line = chip_decay(y, 0, h)
-                for z in (1, 2, 3):
-                    line = line + chip_decay(y, z, h)
-                ahead = y < here.y if way == 0 else y > here.y
-                total = jnp.where(ahead, y_in[way, y, i].astype(F32) + jnp.exp(line) * total, total)
-            for z in order:
-                results[way, z, i] = total.astype(BF16)
-                total = z_in[way, z, i].astype(F32) + jnp.exp(chip_decay(here.y, z, h)) * total
-        for d in (1, 2, 3):
-            wires.send(("r", way, d), results.at[way, turn_z[d]], r_in.at[way, here.z], here.at(z=turn_z[d]))
-        r_in[way, here.z] = results[way, here.z]
-        yield
-        for d in (1, 2, 3):
-            wires.arrived(("r", way, d), r_in.at[way, turn_z[4 - d]])
+            for piece in range(8):
+                totals[way, 2 * piece + i // 3, i % 3] = whole[piece]
+        for dy, dz in apart:
+            wires.send(
+                ("t", way, dy, dz),
+                totals.at[way, chip_at(dy, dz)],
+                t_in.at[way, here.chip],
+                here.at(y=turn_y[dy], z=turn_z[dz]),
+            )
+        t_in[way, here.chip] = totals[way, here.chip]
+        yield
+        for dy, dz in reversed(apart):
+            wires.arrived(("t", way, dy, dz), t_in.at[way, chip_at(-dy, -dz)])
+        for i in range(3):
+            h = core * HALF_HEADS + 3 * lax.rem(here.chip, 2) + i
+            total = jnp.zeros((16, HD), F32)
+            for n in order:
+                results[way, n, i] = total.astype(BF16)
+                decayed = jnp.exp(log_total(2 * n, h) + log_total(2 * n + 1, h))
+                total = t_in[way, n, i].astype(F32) + decayed * total
+        for dy, dz in apart:
+            wires.send(
+                ("r", way, dy, dz),
+                results.at[way, chip_at(dy, dz)],
+                r_in.at[way, here.chip],
+                here.at(y=turn_y[dy], z=turn_z[dz]),
+            )
+        r_in[way, here.chip] = results[way, here.chip]
+        yield
+        for dy, dz in reversed(apart):
+            wires.arrived(("r", way, dy, dz), r_in.at[way, chip_at(-dy, -dz)])
         for i, h in enumerate(heads):
             s_even, s_odd = both_states(i)
-            enters = jnp.stack([r_in[way, quarter, i] for quarter in range(4)], axis=0).astype(F32)
+            enters = jnp.stack([r_in[way, 2 * piece + i // 3, i % 3] for piece in range(8)], axis=0).astype(F32)
             if way == 0:
                 at_even, at_odd = enters, s_even + jnp.exp(log_total(even, h)) * enters
             else:
@@ -332,6 +343,7 @@
         at = slice(h * HD, (h + 1) * HD)
         scaled[0, :, at] = (tails[:, h : h + 1] * k_ref[:, at].astype(F32)).astype(BF16)
         scaled[1, :, at] = (jnp.exp(turned[:, h : h + 1]) * q_ref[:, at].astype(F32)).astype(BF16)
+    to_owner(2)
     earlier = scan(0, v_ref)
     next(earlier)
 
@@ -434,13 +446,16 @@
     pull0, pull1 = gather(0), gather(1)
     next(pull0)
     enter(1)
-    next(pull1)
-    next(earlier)
-    next(pull0)
-    next(pull0)
-    next(pull1)
-    next(pull1)
-    next(pull0)
+    next(pull0)
+    next(pull1)
+    next(pull0)
+    next(pull0)
+    early_sends = len(wires.sent)
+    next(pull0)
+    next(pull0)
+    next(pull1)
+    next(pull0)
+    next(pull1)
     next(pull1)
     for d in (1, 2, 3):
         wires.arrived(("dz", d), decay.at[pl.ds((here.y * 4 + turn_z[4 - d]) * 2, 2)])
@@ -449,15 +464,12 @@
         wires.send(("dy", d), line_of_blocks, line_of_blocks, here.at(y=turn_y[d]))
     next(pull0)
     next(pull0)
-    next(pull1)
-    next(pull1)
-    next(pull0)
-    next(pull1)
-    next(pull0)
-    next(pull0)
-    next(pull0)
-    next(pull0)
-    next(pull1)
+    next(pull0)
+    next(pull1)
+    next(pull1)
+    next(pull0)
+    next(pull1)
+    wires.drain(early_sends)
     next(pull0)
 
     r0, r1 = iota((MAIN, MAIN), 0), iota((MAIN, MAIN), 1)
@@ -474,12 +486,10 @@
 
     def contract(turn, start, stop):
         def one(j, _):
-            at = pl.ds(aligned(pairs[turn] * PAIR + j * 512, 128), 512)
-            to = pl.ds(aligned(pairs[turn] * 2 * QUARTER + j * 512, 512), 512)
-            inputs, grads = rows[0, :, at], rows[1, :, at]
-            acc[0] += dot(inputs, wg[to, :])
-            acc[1] += dot(inputs, wu[to, :])
-            acc[2] += dot_nt(grads, wd[:, to])
+            at = pl.ds(aligned(pairs[turn] * PAIR + j * 1024, 128), 1024)
+            to = pl.ds(aligned(pairs[turn] * 2 * QUARTER + j * 1024, 1024), 1024)
+            acc[...] += dot(rows[0, :, at], wgu[to, :])
+            acc_down[...] += dot_nt(rows[1, :, at], wd[:, to])
             return 0
 
         lax.fori_loop(start, stop, one, 0)
@@ -496,53 +506,51 @@
     for load in loads:
         load.wait()
     acc[...] = jnp.zeros_like(acc)
+    acc_down[...] = jnp.zeros_like(acc_down)
     unfold(0)
-    contract(0, 0, 2)
-    next(pull1)
-    contract(0, 2, 4)
-    next(pull1)
-    contract(0, 4, 6)
+    contract(0, 0, 1)
+    next(pull1)
+    next(pull1)
+    contract(0, 1, 2)
+    next(pull1)
+    contract(0, 2, 3)
     next(pull1)
     for d in (1, 2, 3):
         wires.arrived(("dy", d), decay.at[pl.ds(turn_y[4 - d] * 8, 8)])
     next(earlier)
     next(pull1)
     unfold(1)
-    contract(1, 0, 6)
+    contract(1, 0, 3)
     wires.drain()
-    gate_pre, up_pre, hidden_grad = acc[0], acc[1], acc[2]
+    gate_pre, up_pre, hidden_grad = acc[:, 0:HID], acc[:, HID:], acc_down[...]
     sig = jax.nn.sigmoid(gate_pre)
     active = gate_pre * sig
     hidden[...] = (active * up_pre).astype(BF16)
     acts[:, 0:HID] = (hidden_grad * up_pre * sig * (1.0 + gate_pre * (1.0 - sig))).astype(BF16)
     acts[:, HID:] = (hidden_grad * active).astype(BF16)
 
-    parts, theirs = (part0, part1), (theirs0, theirs1)
-
     def slot_part(which, owner, chunk):
         y_step, z_step = jnp.where(owner == 0, 4, 1), jnp.where(owner == 0, 1, 4)
         part = parts[chunk]
-
-        def one(j, _):
-            q = 2 * chunk + j
+        for j, q in enumerate(QUARTERS[chunk]):
             at = pl.ds(aligned(q * QUARTER + owner * 768, 768), 768)
-            piece = dot_nt(acts[:, 0:HID], wg[at, :]) + dot_nt(acts[:, HID:], wu[at, :])
-            piece = piece.astype(BF16)
-            columns = pl.ds(aligned(j * 768, 768), 768)
+            piece = dot_nt(acts[...], wgu[at, :]).astype(BF16)
             for k in range(16):
                 to = ((k // 4) * y_step + (k % 4) * z_step) * 16
-                part[which, pl.ds(aligned(to, 16), 16), columns] = piece[16 * k : 16 * (k + 1), :]
+                part[which, pl.ds(aligned(to, 16), 16), 768 * j : 768 * (j + 1)] = piece[16 * k : 16 * (k + 1), :]
             for b in range(2):
-                fold[which, pl.ds(aligned((q * 2 + b) * 32, 32), 32), :] = piece[MAIN:, 384 * b : 384 * (b + 1)]
-            return 0
-
-        lax.fori_loop(0, 2, one, 0)
-        if chunk:
+                g = 2 * q + b
+                fold[which, 32 * g : 32 * (g + 1), :] = piece[MAIN:, 384 * b : 384 * (b + 1)]
+        if chunk == 2:
             position, inside = lax.div(r0, 16), lax.rem(r0, 16)
             chip = jnp.where(owner == 0, position, lax.rem(position, 4) * 4 + lax.div(position, 4))
             source = lax.rem(inside, 8) * 32 + chip * 2 + lax.div(inside, 8)
             refold = jnp.where(r1 == source, 1.0, 0.0).astype(BF16)
-            part[which, :, 1536:] = dot(refold, fold[which]).astype(BF16)
+            part[which, :, 768:] = dot(refold, fold[which]).astype(BF16)
+
+    def slots_for_sibling(chunk):
+        slot_part(1, other, chunk)
+        wires.send(("p", chunk), parts[chunk].at[1], theirs[chunk], here.sibling())
 
     def join(chunk):
         wires.arrived(("p", chunk), theirs[chunk])
@@ -586,6 +594,21 @@
         result[...] = (buffer[at, :].astype(F32) + in_m[...].astype(F32) + in_p[...].astype(F32)).astype(BF16)
         yield
 
+    def far_direct(tag, buffer, height, places, device, in_q, in_m, in_p, result):
+        def block(i):
+            return pl.ds(aligned(places[i] * height, height), height)
+
+        for d, landing in ((2, in_q), (1, in_m), (3, in_p)):
+            wires.send((tag, d), buffer.at[block(d), :], landing, device(places[d]))
+        yield
+        yield
+        total = buffer[block(0), :].astype(F32)
+        for d, landing in ((1, in_m), (3, in_p), (2, in_q)):
+            wires.arrived((tag, d), landing)
+            total = total + landing[...].astype(F32)
+        result[...] = total.astype(BF16)
+        yield
+
     def direct_sum(tag, buffer, places, device, landing, result):
         def block(i):
             return pl.ds(aligned(places[i] * 16, 16), 16)
@@ -600,39 +623,50 @@
         result[...] = total.astype(BF16)
         yield
 
-    far0 = ring_sum("r0", part0.at[0], 64, CHUNK_CUTS[0], ss, on_second, a0, b0, m0, p0, group0)
-    far1 = ring_sum("r1", part1.at[0], 64, CHUNK_CUTS[1], ss, on_second, a1, b1, m1, p1, group1)
-    near0 = direct_sum("n0", group0, fs, on_first, landing0, final0)
-    near1 = direct_sum("n1", group1, fs, on_first, landing1, final1)
-    slot_part(1, other, 0)
-    wires.send(("p", 0), part0.at[1], theirs0, here.sibling())
+    far = [
+        ring_sum(
+            ("f", n), parts[n].at[0], 64, CHUNK_CUTS[n], ss, on_second,
+            in_as[n], in_bs[n], in_ms[n], in_ps[n], groups[n],
+        )
+        for n in range(2)
+    ]
+    far.append(far_direct(("f", 2), parts[2].at[0], 64, ss, on_second, in_as[2], in_ms[2], in_ps[2], groups[2]))
+    near = [direct_sum(("n", n), groups[n], fs, on_first, landings[n], sums[n]) for n in range(3)]
+    slots_for_sibling(0)
     slot_part(0, core, 0)
-    slot_part(1, other, 1)
-    wires.send(("p", 1), part1.at[1], theirs1, here.sibling())
+    slots_for_sibling(1)
     join(0)
-    next(far0)
+    next(far[0])
     slot_part(0, core, 1)
     join(1)
-    next(far1)
-    next(far0)
-    next(far1)
-    next(far0)
-    next(near0)
-    next(far1)
-    next(near1)
-    next(near0)
-    next(near1)
-
+    next(far[1])
+    slots_for_sibling(2)
+    slot_part(0, core, 2)
+    next(far[0])
+    join(2)
+    next(far[2])
+    next(far[1])
+    next(far[0])
+    next(near[0])
+    next(far[2])
+    next(far[1])
+    next(near[1])
+    next(far[2])
+    next(near[2])
+    next(near[0])
+    next(near[1])
+    next(near[2])
+    wires.drain(len(wires.sent) - 9)
     own_back = pl.ds(aligned(here.x * 16, 16), 16)
-    back_main = [final0.at[:, 0:768], final0.at[:, 768:1536], final1.at[:, 0:768], final1.at[:, 768:1536]]
     for q in range(4):
-        outgoing[16 * q : 16 * (q + 1), :] = back_main[q][...]
+        n, j = ((0, 0), (1, 0), (1, 1), (2, 0))[q]
+        outgoing[16 * q : 16 * (q + 1), :] = sums[n][:, 768 * j : 768 * (j + 1)]
     for d in (1, 2, 3):
         source = outgoing.at[pl.ds(aligned(across[d] * 16, 16), 16), :]
         wires.send(("b", d), source, back.at[core, own_back, 0:768], here.at(x=across[d]))
-        wires.send(("br", d), final1.at[:, 1536:], back.at[core, own_back, 768:], here.at(x=across[d]))
+        wires.send(("br", d), sums[2].at[:, 768:], back.at[core, own_back, 768:], here.at(x=across[d]))
     back[core, own_back, 0:768] = outgoing[own_back, :]
-    back[core, own_back, 768:] = final1[:, 1536:]
+    back[core, own_back, 768:] = sums[2][:, 768:]
     next(earlier)
     weight_grads(0, 2)
     for d in (1, 2, 3):
@@ -679,9 +713,9 @@
     next(later)
     for h in range(6, HEADS):
         within(h)
+    weight_grads(3, 5)
     next(later)
-    weight_grads(3, 6)
-    next(later)
+    weight_grads(5, 6)
     next(later)
     state_out[...] = final[1]
     wires.drain()
@@ -731,25 +765,19 @@
 
 
 def main_call(ids, route_gates, log_decay, moe_input, out_grad, queries, keys, values, w_gate, w_up, w_down):
-    half = (2, HALF_HEADS, 4, 32, HD)
-    piece = (2, 4, HALF_HEADS, 32, HD)
-    wide = (2, HEADS, 4, 32, HD)
-
-    def ring(width, cut):
-        return [(64, cut), (64, width - cut), (64, width), (64, width), (64, width), (4, 16, width)]
+    half = (2, HALF_HEADS, 8, 16, HD)
+    piece = (2, 16, 3, 16, HD)
+    wide = (2, HEADS, 8, 16, HD)
 
     bf16_scratch = (
         [(ROWS, QUARTER)] * 5
-        + [(D, HID), (D, HID), (HID, D), (2, SLOTS, WIDE), (2, 64, QUARTER + 384), (64, QUARTER + 384), (4, 16, 384)],
+        + [(D, 2 * HID), (HID, D), (2, SLOTS, WIDE), (2, 64, QUARTER + 384), (64, QUARTER + 384), (4, 16, 384)],
         [(SLOTS, HID), (SLOTS, 2 * HID)]
-        + [(2, MAIN, CHUNKS[0]), (2, MAIN, CHUNKS[1]), (MAIN, CHUNKS[0]), (MAIN, CHUNKS[1]), (2, MAIN, 384)]
-        + ring(CHUNKS[0], CHUNK_CUTS[0])
-        + ring(CHUNKS[1], CHUNK_CUTS[1])
-        + [(16, CHUNKS[0]), (16, CHUNKS[1]), (64, 768), (2, 64, 1152)],
-        [(2, ROWS, QUARTER), (ROWS, QUARTER), wide, half, piece, piece, piece, piece, piece, half, wide],
+        + [(2, MAIN, 384), (64, 768), (2, 64, 1152)],
+        [(2, ROWS, QUARTER), (ROWS, QUARTER), wide, half, piece, piece, piece, piece, half, wide],
     )
     f32_scratch = (
-        [(3, SLOTS, HID)],
+        [(SLOTS, 2 * HID), (SLOTS, HID)],
         [(32, 16, ROWS), (16, ROWS), (ROWS, ROWS)],
         [],
     )
@@ -757,6 +785,13 @@
     for narrow, broad in zip(bf16_scratch, f32_scratch):
         scratch += [pltpu.VMEM(dims, BF16) for dims in narrow]
         scratch += [pltpu.VMEM(dims, F32) for dims in broad]
+    for n, (width, cut) in enumerate(zip(CHUNKS, CHUNK_CUTS)):
+        firsts = ((64, cut), (64, width - cut)) if n < 2 else ((64, width), (16, 128))
+        for dims in (
+            (2, MAIN, width), (MAIN, width), *firsts, (64, width), (64, width),
+            (64, width), (4, 16, width), (16, width),
+        ):
+            scratch.append(pltpu.VMEM(dims, BF16))
     return pl.pallas_call(
         main_kernel,
         out_shape=(
@@ -765,7 +800,7 @@
             pltpu.VMEM((HID, D), BF16),
             pltpu.VMEM((ROWS, QUARTER), BF16),
             pltpu.VMEM((2, ROWS, QUARTER), F32),
-            pltpu.VMEM((HEADS, 4, 32, HD), BF16),
+            pltpu.VMEM((HEADS, 8, 16, HD), BF16),
             pltpu.VMEM((ROWS, ROWS), F32),
         ),
         in_specs=[pl.BlockSpec(memory_space=pltpu.HBM)] * 11,

time: 93.9 us -> 90.6 us (0.965)
  Pallas kernels: 93 us -> 89.6 us
    pallas_call x1, Pallas kernels: 88.5 us -> 85.2 us  [main_call(): pl.pallas_call(main_kernel, out_shape=(pltpu.VMEM((D, HID), BF16), pltpu....]
where the time goes in v3:
time: 90.6 us; the launch traced here: 90.5 us
  Pallas kernels  89.6 us (99%)
    pallas_call x1, Pallas kernels, main_call(): pl.pallas_call(main_kernel, out_shape=(pltpu.VMEM((D, HID), BF16), pltpu....  85.2 us
    pallas_call x1, Pallas kernels, last_call(): pl.pallas_call(last_kernel, out_shape=tuple((shape(dims) for dims in outp...  4.44 us

profile of v3, /device:TPU:1, one launch (start us, length us, event | category | flops | bytes accessed | tf_op | source)
XLA Modules:
  0.0 90.5 jit_solution(14320011559522946101)
XLA Ops:
  0.6 0.0 copy-start
  0.6 0.0 copy-start.1
  0.7 85.2 %routed_experts_and_scans.1 = (bf16[6144,256]{1,0:T(8,128)(2,1)S(1)}, bf16[6144,256]{1,0:T(8,128)(2,1)S(1)}, bf16[256,6144]{1,0:T(8,128)(2,1)S(1)}, bf16[128,153...) custom-call(s32[2,128]{1,0:T(2,128)} %bitcast.11, ...), custom_call_target="tpu_custom_call" | custom-call | tf_op jit(solution)/shard_map/routed_experts_and_scans/pallas_call | solution.py:795
  85.8 0.0 copy-done
  85.9 0.0 copy-done.1
  85.9 4.4 %outputs.1 = (bf16[6144,256]{1,0:T(8,128)(2,1)}, bf16[6144,256]{1,0:T(8,128)(2,1)}, bf16[256,6144]{1,0:T(8,128)(2,1)}, bf16[128,1536]{1,0:T(8,128)(2,1)}, bf16[1...) custom-call(bf16[6144,256]{1,0:T(8,128)(2,1)S(1)} %get-tuple-element.19.gate_ref, ...), custom_call_target="tpu_custom_call" | custom-call | tf_op jit(solution)/shard_map/outputs/pallas_call | solution.py:829
Async XLA Ops:
  0.6 85.2 %copy-start = (bf16[128,1536]{1,0:T(8,128)(2,1)S(1)}, bf16[128,1536]{1,0:T(8,128)(2,1)}, u32[]{:S(2)}) copy-start(bf16[128,1536]{1,0:T(8,128)(2,1)} %k_hbm.3) | copy-start | bytes 1179652
  0.6 85.2 %copy-start.1 = (bf16[128,1536]{1,0:T(8,128)(2,1)S(1)}, bf16[128,1536]{1,0:T(8,128)(2,1)}, u32[]{:S(2)}) copy-start(bf16[128,1536]{1,0:T(8,128)(2,1)} %v_hbm.3) | copy-start | bytes 1179652

commit v4 on v3

--- a/solution.py
+++ b/solution.py
@@ -25,7 +25,7 @@
 QUARTERS = ((0,), (1, 2), (3,))
 CHUNKS = (768, 1536, 1152)
 CHUNK_CUTS = (384, 768, 640)
-SENDS = 81
+SENDS = 77
 RECEIVES = 182
 BIG = 42 * 1024 * 1024
 
@@ -446,8 +446,8 @@
     pull0, pull1 = gather(0), gather(1)
     next(pull0)
     enter(1)
-    next(pull0)
-    next(pull1)
+    next(pull1)
+    next(pull0)
     next(pull0)
     next(pull0)
     early_sends = len(wires.sent)
@@ -468,31 +468,43 @@
     next(pull1)
     next(pull1)
     next(pull0)
-    next(pull1)
     wires.drain(early_sends)
     next(pull0)
 
     r0, r1 = iota((MAIN, MAIN), 0), iota((MAIN, MAIN), 1)
 
-    def unfold(turn):
+    def unfold(turn, which):
         chip_core, grp = lax.rem(r0, 32), lax.div(r0, 32)
         select = jnp.where(r1 == chip_core * 8 + grp, 1.0, 0.0).astype(BF16)
         base = pairs[turn] * PAIR
-        for which in range(2):
-            spread = dot(select, rows[which, 0:MAIN, pl.ds(aligned(base + 2 * QUARTER, 128), 384)]).astype(BF16)
-            for g in range(8):
-                at = pl.ds(aligned(base + g * 384, 128), 384)
-                rows[which, MAIN:SLOTS, at] = spread[32 * g : 32 * (g + 1), :]
-
-    def contract(turn, start, stop):
+        spread = dot(select, rows[which, 0:MAIN, pl.ds(aligned(base + 2 * QUARTER, 128), 384)]).astype(BF16)
+        for g in range(8):
+            at = pl.ds(aligned(base + g * 384, 128), 384)
+            rows[which, MAIN:SLOTS, at] = spread[32 * g : 32 * (g + 1), :]
+
+    def depth(turn, j):
+        at = pl.ds(aligned(pairs[turn] * PAIR + j * 1024, 128), 1024)
+        return at, pl.ds(aligned(pairs[turn] * 2 * QUARTER + j * 1024, 1024), 1024)
+
+    def contract_inputs(turn, start=0, stop=3):
         def one(j, _):
-            at = pl.ds(aligned(pairs[turn] * PAIR + j * 1024, 128), 1024)
-            to = pl.ds(aligned(pairs[turn] * 2 * QUARTER + j * 1024, 1024), 1024)
+            at, to = depth(turn, j)
             acc[...] += dot(rows[0, :, at], wgu[to, :])
+            return 0
+
+        lax.fori_loop(start, stop, one, 0)
+
+    def contract_grads(turn, start=0, stop=3):
+        def one(j, _):
+            at, to = depth(turn, j)
             acc_down[...] += dot_nt(rows[1, :, at], wd[:, to])
             return 0
 
         lax.fori_loop(start, stop, one, 0)
+
+    def contract(turn, start, stop):
+        contract_inputs(turn, start, stop)
+        contract_grads(turn, start, stop)
 
     def weight_grads(start, stop):
         for i in range(start, stop):
@@ -507,20 +519,26 @@
         load.wait()
     acc[...] = jnp.zeros_like(acc)
     acc_down[...] = jnp.zeros_like(acc_down)
-    unfold(0)
+    unfold(0, 0)
+    unfold(0, 1)
     contract(0, 0, 1)
     next(pull1)
-    next(pull1)
     contract(0, 1, 2)
+    next(pull1)
+    next(pull1)
     next(pull1)
     contract(0, 2, 3)
     next(pull1)
     for d in (1, 2, 3):
         wires.arrived(("dy", d), decay.at[pl.ds(turn_y[4 - d] * 8, 8)])
     next(earlier)
-    next(pull1)
-    unfold(1)
-    contract(1, 0, 3)
+    unfold(1, core)
+    pl.when(core == 0)(lambda: contract_inputs(1))
+    pl.when(core == 1)(lambda: contract_grads(1))
+    next(pull1)
+    unfold(1, other)
+    pl.when(core == 0)(lambda: contract_grads(1))
+    pl.when(core == 1)(lambda: contract_inputs(1))
     wires.drain()
     gate_pre, up_pre, hidden_grad = acc[:, 0:HID], acc[:, HID:], acc_down[...]
     sig = jax.nn.sigmoid(gate_pre)

time: 90.6 us -> 89.3 us (0.986)
  Pallas kernels: 89.6 us -> 88.4 us
    pallas_call x1, Pallas kernels: 85.2 us -> 83.9 us  [main_call(): pl.pallas_call(main_kernel, out_shape=(pltpu.VMEM((D, HID), BF16), pltpu....]
where the time goes in v4:
time: 89.3 us; the launch traced here: 89.2 us
  Pallas kernels  88.4 us (99%)
    pallas_call x1, Pallas kernels, main_call(): pl.pallas_call(main_kernel, out_shape=(pltpu.VMEM((D, HID), BF16), pltpu....  83.9 us
    pallas_call x1, Pallas kernels, last_call(): pl.pallas_call(last_kernel, out_shape=tuple((shape(dims) for dims in outp...  4.44 us

profile of v4, /device:TPU:1, one launch (start us, length us, event | category | flops | bytes accessed | tf_op | source)
XLA Modules:
  0.0 89.2 jit_solution(4164092663261004895)
XLA Ops:
  0.6 0.0 copy-start
  0.6 0.0 copy-start.1
  0.7 83.9 %routed_experts_and_scans.1 = (bf16[6144,256]{1,0:T(8,128)(2,1)S(1)}, bf16[6144,256]{1,0:T(8,128)(2,1)S(1)}, bf16[256,6144]{1,0:T(8,128)(2,1)S(1)}, bf16[128,153...) custom-call(s32[2,128]{1,0:T(2,128)} %bitcast.11, ...), custom_call_target="tpu_custom_call" | custom-call | tf_op jit(solution)/shard_map/routed_experts_and_scans/pallas_call | solution.py:813
  84.6 0.0 copy-done
  84.6 0.0 copy-done.1
  84.6 4.4 %outputs.1 = (bf16[6144,256]{1,0:T(8,128)(2,1)}, bf16[6144,256]{1,0:T(8,128)(2,1)}, bf16[256,6144]{1,0:T(8,128)(2,1)}, bf16[128,1536]{1,0:T(8,128)(2,1)}, bf16[1...) custom-call(bf16[6144,256]{1,0:T(8,128)(2,1)S(1)} %get-tuple-element.19.gate_ref, ...), custom_call_target="tpu_custom_call" | custom-call | tf_op jit(solution)/shard_map/outputs/pallas_call | solution.py:847
Async XLA Ops:
  0.6 84.0 %copy-start = (bf16[128,1536]{1,0:T(8,128)(2,1)S(1)}, bf16[128,1536]{1,0:T(8,128)(2,1)}, u32[]{:S(2)}) copy-start(bf16[128,1536]{1,0:T(8,128)(2,1)} %k_hbm.3) | copy-start | bytes 1179652
  0.6 84.0 %copy-start.1 = (bf16[128,1536]{1,0:T(8,128)(2,1)S(1)}, bf16[128,1536]{1,0:T(8,128)(2,1)}, u32[]{:S(2)}) copy-start(bf16[128,1536]{1,0:T(8,128)(2,1)} %v_hbm.3) | copy-start | bytes 1179652
